TPU v7x, 32 devices: a whole 2x2x4 slice. The times are simulated.
32 devices in a mesh: seq: 8 (over z, y), tp: 4 (over x, core).
Axes of the slice: x: 2, y: 2, z: 4, core: 2. Of those that a mesh axis runs over, the one named last changes fastest.
Arguments:
- att_query: bfloat16 [1024, 8192], P('seq', 'tp'), may hold values from -12 to 12
- att_key: bfloat16 [1024, 8192], P('seq', 'tp'), may hold values from -6 to 6
- att_value: bfloat16 [1024, 8192], P('seq', 'tp'), may hold values from -6 to 6
- past_key: bfloat16 [256, 8192], P(('seq', 'tp')), may hold values from -6 to 6
- past_value: bfloat16 [256, 8192], P(('seq', 'tp')), may hold values from -6 to 6
Outputs:
- attn_out: bfloat16 [1024, 8192], P('seq', 'tp')
All inputs are finite; a program needn't handle non-finite values.
Results may differ from a plain program's by a relative error of at most 0.006.
Values may be sent and summed in bfloat16 or wider, within the bound.
A program may use at most 128 MiB of HBM per device.

v0:
```python
import jax
import jax.numpy as jnp
from jax import lax
from jax.sharding import PartitionSpec as P

HEAD = 128


NEGATIVE = -1e30


def split_heads(block):
    return block.reshape(block.shape[0], block.shape[1] // HEAD, HEAD)


def absorb(state, queries, query_pos, keys, values, key_pos):
    maxima, totals, sums = state
    scores = jnp.einsum(
        "hqd,khd->hqk", queries, keys, preferred_element_type=jnp.float32
    ) * HEAD ** (-0.5)
    allowed = key_pos[None, None, :] <= query_pos[None, :, None]
    scores = jnp.where(allowed, scores, NEGATIVE)
    newmax = jnp.maximum(maxima, jnp.max(scores, axis=2))
    factor = jnp.exp(maxima - newmax)
    weights = jnp.where(allowed, jnp.exp(scores - newmax[:, :, None]), 0.0)
    totals = totals * factor + jnp.sum(weights, axis=2)
    sums = sums * factor[:, :, None] + jnp.einsum(
        "hqk,khd->hqd", weights.astype(jnp.bfloat16), values, preferred_element_type=jnp.float32
    )
    return (newmax, totals, sums)


def absorb_when_needed(state, queries, query_pos, keys, values, key_pos):
    return lax.cond(
        jnp.min(key_pos) > jnp.max(query_pos),
        lambda carried: carried,
        lambda carried: absorb(carried, queries, query_pos, keys, values, key_pos),
        state,
    )


def finish(state):
    maxima, totals, sums = state
    result = sums / totals[:, :, None]
    return jnp.transpose(result, (1, 0, 2)).reshape(result.shape[1], -1).astype(jnp.bfloat16)


def empty_state(head_count, count):
    return (
        jnp.full((head_count, count), NEGATIVE, jnp.float32),
        jnp.zeros((head_count, count), jnp.float32),
        jnp.zeros((head_count, count, HEAD), jnp.float32),
    )


def local(att_query, att_key, att_value, past_key, past_value):
    seq_count = lax.axis_size("seq")
    position = lax.axis_index("seq")
    past_keys, past_values = (
        lax.all_to_all(past_key, "tp", split_axis=1, concat_axis=0, tiled=True),
        lax.all_to_all(past_value, "tp", split_axis=1, concat_axis=0, tiled=True),
    )
    past_rows = past_keys.shape[0]
    hist_total = past_rows * seq_count
    rows = att_query.shape[0]
    heads_here = att_query.shape[1] // HEAD
    per_device = max(1, heads_here // seq_count)
    repeat = max(1, seq_count // heads_here)
    span = past_rows + rows

    def spread(block):
        return jnp.tile(split_heads(block), (1, repeat, 1))

    stacked_keys = jnp.concatenate([past_keys, att_key], 0)
    stacked_values = jnp.concatenate([past_values, att_value], 0)
    got_query, got_keys, got_values = (
        lax.all_to_all(spread(att_query), "seq", split_axis=1, concat_axis=0, tiled=True),
        lax.all_to_all(spread(stacked_keys), "seq", split_axis=1, concat_axis=0, tiled=True),
        lax.all_to_all(spread(stacked_values), "seq", split_axis=1, concat_axis=0, tiled=True),
    )
    stretch_total = rows * seq_count
    copy_index = position // heads_here
    piece = stretch_total // (2 * repeat)
    first_start = copy_index * piece
    second_start = (2 * repeat - 1 - copy_index) * piece
    offsets = jnp.arange(piece, dtype=jnp.int32)
    pos_one = hist_total + first_start + offsets
    pos_two = hist_total + second_start + offsets
    query_one = jnp.transpose(lax.dynamic_slice_in_dim(got_query, first_start, piece, 0), (1, 0, 2))
    query_two = jnp.transpose(
        lax.dynamic_slice_in_dim(got_query, second_start, piece, 0), (1, 0, 2)
    )
    source = jnp.arange(seq_count, dtype=jnp.int32)[:, None]
    within = jnp.arange(span, dtype=jnp.int32)[None, :]
    key_table = jnp.where(
        within < past_rows,
        source * past_rows + within,
        hist_total + source * rows + within - past_rows,
    )
    turns = seq_count // 2
    key_blocks = got_keys.reshape(turns, 2 * span, per_device, HEAD)
    value_blocks = got_values.reshape(turns, 2 * span, per_device, HEAD)
    pos_blocks = key_table.reshape(turns, 2 * span)

    def step_block(carry_now, items):
        keys, values, key_pos = items
        return (
            (
                absorb_when_needed(carry_now[0], query_one, pos_one, keys, values, key_pos),
                absorb_when_needed(carry_now[1], query_two, pos_two, keys, values, key_pos),
            ),
            None,
        )

    start_state = empty_state(per_device, piece)
    carry, unused = lax.scan(
        step_block, (start_state, start_state), (key_blocks, value_blocks, pos_blocks)
    )
    placed = jnp.zeros((stretch_total, per_device * HEAD), jnp.bfloat16)
    placed = lax.dynamic_update_slice_in_dim(placed, finish(carry[0]), first_start, 0)
    placed = lax.dynamic_update_slice_in_dim(placed, finish(carry[1]), second_start, 0)
    returned = lax.all_to_all(
        placed.reshape(stretch_total, per_device, HEAD),
        "seq",
        split_axis=0,
        concat_axis=1,
        tiled=True,
    )
    summed = jnp.sum(returned.reshape(rows, repeat, heads_here, HEAD).astype(jnp.float32), axis=1)
    return summed.reshape(rows, heads_here * HEAD).astype(jnp.bfloat16)


def solution(mesh):
    placed = (
        P("seq", "tp"),
        P("seq", "tp"),
        P("seq", "tp"),
        P(("seq", "tp"), None),
        P(("seq", "tp"), None),
    )
    return jax.shard_map(
        local, mesh=mesh, in_specs=placed, out_specs=P("seq", "tp"), check_vma=False
    )
```

profile of v0, /device:TPU:0, one launch (start us, length us, event | category | flops | bytes accessed | tf_op | source)
XLA Modules:
  0.0 126.5 jit_solution(5401712648746760187)
XLA Ops:
  0.0 9.0 %all_to_all.95 = bf16[8,4,2048]{2,0,1:T(8,128)(2,1)S(1)} all-to-all(bf16[8,4,2048]{2,0,1:T(8,128)(2,1)} %bitcast.73), channel_id=1, replica_groups=mesh['seq'=8,'tp'=4] {'tp'}, dimensions={1} | all-to-all | bytes 262144 | tf_op jit(solution)/shard_map/all_to_all | solution.py:61
  9.0 3.3 %all-to-all-start = ((bf16[8,4,2048]{2,0,1:T(8,128)(2,1)}), bf16[8,4,2048]{2,0,1:T(8,128)(2,1)S(1)}, u32[]{:S(2)}, u32[]{:S(2)}) async-start(bf16[8,4,2048]{2,0,1:T(8,128)(2,1)} %bitcast.74), calls=%async_computation | async-start | bytes 262144 | tf_op jit(solution)/shard_map/all_to_all | solution.py:60
  12.3 2.0 %copy.48 = bf16[128,2048]{0,1:T(8,128)(2,1)} copy(bf16[128,2048]{1,0:T(8,128)(2,1)} %param.11) | data formatting | bytes 1048576 | tf_op args[0]
  14.4 2.6 %all-to-all-done = bf16[8,4,2048]{2,0,1:T(8,128)(2,1)S(1)} async-done(((bf16[8,4,2048]{2,0,1:T(8,128)(2,1)}), bf16[8,4,2048]{2,0,1:T(8,128)(2,1)S(1)}, u32[]{:S(2)}, u32[]{:S(2)}) %all-to-all-start) | async-done | bytes 131104 | tf_op jit(solution)/shard_map/all_to_all | solution.py:60
  16.9 6.4 %all-to-all-start.4 = ((bf16[128,16,128]{0,2,1:T(8,128)(2,1)}), bf16[128,16,128]{0,2,1:T(8,128)(2,1)S(1)}, u32[]{:S(2)}, u32[]{:S(2)}) async-start(bf16[128,16,128]{0,2,1:T(8,128)(2,1)} %bitcast.12), calls=%async_computation.4 | async-start | bytes 1048576 | tf_op jit(solution)/shard_map/all_to_all | solution.py:77
  24.4 1.3 copy.46
  25.6 11.8 %all-to-all-done.4 = bf16[128,16,128]{0,2,1:T(8,128)(2,1)S(1)} async-done(((bf16[128,16,128]{0,2,1:T(8,128)(2,1)}), bf16[128,16,128]{0,2,1:T(8,128)(2,1)S(1)}, u32[]{:S(2)}, u32[]{:S(2)}) %all-to-all-start.4) | async-done | bytes 524320 | tf_op jit(solution)/shard_map/all_to_all | solution.py:77
  37.4 3.6 %all-to-all-start.3 = ((bf16[160,16,128]{2,0,1:T(8,128)(2,1)}), bf16[160,16,128]{2,0,1:T(8,128)(2,1)S(1)}, u32[]{:S(2)}, u32[]{:S(2)}) async-start(bf16[160,16,128]{2,0,1:T(8,128)(2,1)} %copy.46), calls=%async_computation.3 | async-start | bytes 1310720 | tf_op jit(solution)/shard_map/all_to_all | solution.py:79
  42.2 1.2 copy.42
  43.4 14.9 %all-to-all-done.3 = bf16[160,16,128]{2,0,1:T(8,128)(2,1)S(1)} async-done(((bf16[160,16,128]{2,0,1:T(8,128)(2,1)}), bf16[160,16,128]{2,0,1:T(8,128)(2,1)S(1)}, u32[]{:S(2)}, u32[]{:S(2)}) %all-to-all-start.3) | async-done | bytes 655392 | tf_op jit(solution)/shard_map/all_to_all | solution.py:79
  58.3 3.6 %all-to-all-start.1 = ((bf16[160,16,128]{2,0,1:T(8,128)(2,1)}), bf16[160,16,128]{2,0,1:T(8,128)(2,1)S(1)}, u32[]{:S(2)}, u32[]{:S(2)}) async-start(bf16[160,16,128]{2,0,1:T(8,128)(2,1)} %copy.42), calls=%async_computation.1 | async-start | bytes 1310720 | tf_op jit(solution)/shard_map/all_to_all | solution.py:78
  62.5 0.7 add_reduce_fusion
  63.6 15.9 %all-to-all-done.1 = bf16[160,16,128]{2,0,1:T(8,128)(2,1)S(1)} async-done(((bf16[160,16,128]{2,0,1:T(8,128)(2,1)}), bf16[160,16,128]{2,0,1:T(8,128)(2,1)S(1)}, u32[]{:S(2)}, u32[]{:S(2)}) %all-to-all-start.1) | async-done | bytes 655392 | tf_op jit(solution)/shard_map/all_to_all | solution.py:78
  79.6 26.3 %while.22 = (s32[]{:T(128)}, f32[2,512]{1,0:T(2,128)S(1)}, f32[2,512]{1,0:T(2,128)S(1)}, f32[2,512,128]{2,1,0:T(8,128)S(1)}, f32[2,512]{1,0:T(2,128)S(1)}, /*ind...) while((s32[]{:T(128)}, f32[2,512]{1,0:T(2,128)S(1)}, ...), condition=%wide.region_12.13_spmd.clone, body=%wide.region_2.12_spmd.clone.sunk | while | flops 342299968 | bytes 13260221 | solution.py:116
  81.6 1.6 %conditional.7 = (f32[2,512]{1,0:T(2,128)S(1)}, f32[2,512]{1,0:T(2,128)S(1)}, f32[2,512,128]{2,1,0:T(8,128)S(1)}) conditional(s32[]{:T(128)} %convert_element_type.54, (s32[320]{0:T(512)S(1)}, s32[]{:T(128)}, bf16[2,512,128]{2,1,0:T(8,128)(2,1)S(1)}, bf16[320,2,128]{2,0,1:T(8,128)(2,1)S(1)}, f32[2,512]{1,0:T(2,128)S(1)}, ...), branch_computations={%region_8.10_spmd, %region_11.11_spmd} | conditional | flops 171149824 | bytes 6290716 | solution.py:34
  82.5 0.7 convolution_add_fusion.1
  84.5 1.6 %conditional.6 = (f32[2,512]{1,0:T(2,128)S(1)}, f32[2,512]{1,0:T(2,128)S(1)}, f32[2,512,128]{2,1,0:T(8,128)S(1)}) conditional(s32[]{:T(128)} %convert_element_type.53, (s32[320]{0:T(512)S(1)}, s32[]{:T(128)}, bf16[2,512,128]{2,1,0:T(8,128)(2,1)S(1)}, bf16[320,2,128]{2,0,1:T(8,128)(2,1)S(1)}, f32[2,512]{1,0:T(2,128)S(1)}, ...), branch_computations={%region_4.6_spmd, %region_7.7_spmd} | conditional | flops 171149824 | bytes 6290716 | solution.py:34
  85.5 0.7 convolution_add_fusion
  88.2 1.6 %conditional.7 = (f32[2,512]{1,0:T(2,128)S(1)}, f32[2,512]{1,0:T(2,128)S(1)}, f32[2,512,128]{2,1,0:T(8,128)S(1)}) conditional(s32[]{:T(128)} %convert_element_type.54, (s32[320]{0:T(512)S(1)}, s32[]{:T(128)}, bf16[2,512,128]{2,1,0:T(8,128)(2,1)S(1)}, bf16[320,2,128]{2,0,1:T(8,128)(2,1)S(1)}, f32[2,512]{1,0:T(2,128)S(1)}, ...), branch_computations={%region_8.10_spmd, %region_11.11_spmd} | conditional | flops 171149824 | bytes 6290716 | solution.py:34
  89.1 0.7 convolution_add_fusion.1
  91.1 1.6 %conditional.6 = (f32[2,512]{1,0:T(2,128)S(1)}, f32[2,512]{1,0:T(2,128)S(1)}, f32[2,512,128]{2,1,0:T(8,128)S(1)}) conditional(s32[]{:T(128)} %convert_element_type.53, (s32[320]{0:T(512)S(1)}, s32[]{:T(128)}, bf16[2,512,128]{2,1,0:T(8,128)(2,1)S(1)}, bf16[320,2,128]{2,0,1:T(8,128)(2,1)S(1)}, f32[2,512]{1,0:T(2,128)S(1)}, ...), branch_computations={%region_4.6_spmd, %region_7.7_spmd} | conditional | flops 171149824 | bytes 6290716 | solution.py:34
  92.0 0.7 convolution_add_fusion
  94.8 1.6 %conditional.7 = (f32[2,512]{1,0:T(2,128)S(1)}, f32[2,512]{1,0:T(2,128)S(1)}, f32[2,512,128]{2,1,0:T(8,128)S(1)}) conditional(s32[]{:T(128)} %convert_element_type.54, (s32[320]{0:T(512)S(1)}, s32[]{:T(128)}, bf16[2,512,128]{2,1,0:T(8,128)(2,1)S(1)}, bf16[320,2,128]{2,0,1:T(8,128)(2,1)S(1)}, f32[2,512]{1,0:T(2,128)S(1)}, ...), branch_computations={%region_8.10_spmd, %region_11.11_spmd} | conditional | flops 171149824 | bytes 6290716 | solution.py:34
  95.7 0.7 convolution_add_fusion.1
  97.7 1.6 %conditional.6 = (f32[2,512]{1,0:T(2,128)S(1)}, f32[2,512]{1,0:T(2,128)S(1)}, f32[2,512,128]{2,1,0:T(8,128)S(1)}) conditional(s32[]{:T(128)} %convert_element_type.53, (s32[320]{0:T(512)S(1)}, s32[]{:T(128)}, bf16[2,512,128]{2,1,0:T(8,128)(2,1)S(1)}, bf16[320,2,128]{2,0,1:T(8,128)(2,1)S(1)}, f32[2,512]{1,0:T(2,128)S(1)}, ...), branch_computations={%region_4.6_spmd, %region_7.7_spmd} | conditional | flops 171149824 | bytes 6290716 | solution.py:34
  98.6 0.7 convolution_add_fusion
  101.4 1.6 %conditional.7 = (f32[2,512]{1,0:T(2,128)S(1)}, f32[2,512]{1,0:T(2,128)S(1)}, f32[2,512,128]{2,1,0:T(8,128)S(1)}) conditional(s32[]{:T(128)} %convert_element_type.54, (s32[320]{0:T(512)S(1)}, s32[]{:T(128)}, bf16[2,512,128]{2,1,0:T(8,128)(2,1)S(1)}, bf16[320,2,128]{2,0,1:T(8,128)(2,1)S(1)}, f32[2,512]{1,0:T(2,128)S(1)}, ...), branch_computations={%region_8.10_spmd, %region_11.11_spmd} | conditional | flops 171149824 | bytes 6290716 | solution.py:34
  102.3 0.7 convolution_add_fusion.1
  104.3 1.6 %conditional.6 = (f32[2,512]{1,0:T(2,128)S(1)}, f32[2,512]{1,0:T(2,128)S(1)}, f32[2,512,128]{2,1,0:T(8,128)S(1)}) conditional(s32[]{:T(128)} %convert_element_type.53, (s32[320]{0:T(512)S(1)}, s32[]{:T(128)}, bf16[2,512,128]{2,1,0:T(8,128)(2,1)S(1)}, bf16[320,2,128]{2,0,1:T(8,128)(2,1)S(1)}, f32[2,512]{1,0:T(2,128)S(1)}, ...), branch_computations={%region_4.6_spmd, %region_7.7_spmd} | conditional | flops 171149824 | bytes 6290716 | solution.py:34
  105.2 0.7 convolution_add_fusion
  107.0 18.1 %all_to_all.96 = bf16[1024,2,128]{2,1,0:T(2,128)(2,1)S(1)} all-to-all(bf16[1024,2,128]{2,1,0:T(2,128)(2,1)S(1)} %copy.55), channel_id=1, replica_groups=mesh['seq'=8,'tp'=4] {'seq'}, dimensions={0} | all-to-all | bytes 1048576 | tf_op jit(solution)/shard_map/all_to_all | solution.py:122
  125.5 1.0 copy.58
  (116 shorter events, 14.4 us)
Async XLA Ops:
  0.0 23.3 %copy-start = (bf16[128,2048]{1,0:T(8,128)(2,1)S(1)}, bf16[128,2048]{1,0:T(8,128)(2,1)}, u32[]{:S(2)}) copy-start(bf16[128,2048]{1,0:T(8,128)(2,1)} %param.13) | copy-start | bytes 1572868
  9.0 7.9 %all-to-all-start = ((bf16[8,4,2048]{2,0,1:T(8,128)(2,1)}), bf16[8,4,2048]{2,0,1:T(8,128)(2,1)S(1)}, u32[]{:S(2)}, u32[]{:S(2)}) async-start(bf16[8,4,2048]{2,0,1:T(8,128)(2,1)} %bitcast.74), calls=%async_computation | async-start | bytes 262144 | tf_op jit(solution)/shard_map/all_to_all | solution.py:60
  16.9 20.5 %all-to-all-start.4 = ((bf16[128,16,128]{0,2,1:T(8,128)(2,1)}), bf16[128,16,128]{0,2,1:T(8,128)(2,1)S(1)}, u32[]{:S(2)}, u32[]{:S(2)}) async-start(bf16[128,16,128]{0,2,1:T(8,128)(2,1)} %bitcast.12), calls=%async_computation.4 | async-start | bytes 1048576 | tf_op jit(solution)/shard_map/all_to_all | solution.py:77
  24.4 16.7 %copy-start.1 = (bf16[128,2048]{1,0:T(8,128)(2,1)S(1)}, bf16[128,2048]{1,0:T(8,128)(2,1)}, u32[]{:S(2)}) copy-start(bf16[128,2048]{1,0:T(8,128)(2,1)} %param.12) | copy-start | bytes 1572868
  37.4 20.9 %all-to-all-start.3 = ((bf16[160,16,128]{2,0,1:T(8,128)(2,1)}), bf16[160,16,128]{2,0,1:T(8,128)(2,1)S(1)}, u32[]{:S(2)}, u32[]{:S(2)}) async-start(bf16[160,16,128]{2,0,1:T(8,128)(2,1)} %copy.46), calls=%async_computation.3 | async-start | bytes 1310720 | tf_op jit(solution)/shard_map/all_to_all | solution.py:79
  58.3 21.1 %all-to-all-start.1 = ((bf16[160,16,128]{2,0,1:T(8,128)(2,1)}), bf16[160,16,128]{2,0,1:T(8,128)(2,1)S(1)}, u32[]{:S(2)}, u32[]{:S(2)}) async-start(bf16[160,16,128]{2,0,1:T(8,128)(2,1)} %copy.42), calls=%async_computation.1 | async-start | bytes 1310720 | tf_op jit(solution)/shard_map/all_to_all | solution.py:78
where the time goes:
time: 127 us
  waiting for transfers between devices  45.1 us (36%)
  blocking collectives  27.1 us (21%)
  starting transfers between devices  17 us (13%)
  loops' own time  10.8 us (9%)
  local copies, waits for them, and re-layouts  9.18 us (7%)
  matrix products  8.99 us (7%)
  other arithmetic  8.17 us (6%)
    all_to_all x1, blocking collectives, local(): lax.all_to_all(placed.reshape(stretch_total, per_device, HEAD), 'seq', sp...  18.1 us
    all_to_all x1, waiting for transfers between devices, local(): lax.all_to_all(spread(stacked_keys), 'seq', split_axis=1, concat_axis=0,...  15.9 us
    all_to_all x1, waiting for transfers between devices, local(): lax.all_to_all(spread(stacked_values), 'seq', split_axis=1, concat_axis=0...  14.9 us
    all_to_all x1, waiting for transfers between devices, local(): lax.all_to_all(spread(att_query), 'seq', split_axis=1, concat_axis=0, til...  11.8 us
    another operation x1, loops' own time, local(): lax.scan(step_block, (start_state, start_state), (key_blocks, value_block...  10.3 us
    all_to_all x1, blocking collectives, local(): lax.all_to_all(past_value, 'tp', split_axis=1, concat_axis=0, tiled=True)  8.97 us
    all_to_all x1, starting transfers between devices, local(): lax.all_to_all(spread(att_query), 'seq', split_axis=1, concat_axis=0, til...  6.36 us
    dot_general x8, matrix products, absorb(): jnp.einsum('hqk,khd->hqd', weights.astype(jnp.bfloat16), values, preferre...  5.73 us
  transfers between devices with their start and end apart: 4, of which 4 were waited for; matrix products, arithmetic and copies ran while one was open for 7% of the time, Pallas kernels for 0%

commit v1 on v0

--- a/solution.py
+++ b/solution.py
@@ -1,6 +1,10 @@
+import functools
+
 import jax
 import jax.numpy as jnp
 from jax import lax
+from jax.experimental import pallas as pl
+from jax.experimental.pallas import tpu as pltpu
 from jax.sharding import PartitionSpec as P
 
 HEAD = 128
@@ -53,7 +57,7 @@
     )
 
 
-def local(att_query, att_key, att_value, past_key, past_value):
+def local_xla(att_query, att_key, att_value, past_key, past_value):
     seq_count = lax.axis_size("seq")
     position = lax.axis_index("seq")
     past_keys, past_values = (
@@ -130,6 +134,188 @@
     return summed.reshape(rows, heads_here * HEAD).astype(jnp.bfloat16)
 
 
+def attend(query, past_keys, past_values, keys, values):
+    rows = query.shape[0]
+    contract = (((1,), (1,)), ((), ()))
+    past = lax.dot_general(query, past_keys, contract, preferred_element_type=jnp.float32)
+    here = lax.dot_general(query, keys, contract, preferred_element_type=jnp.float32)
+    free = here.shape[1] - rows
+    down = lax.broadcasted_iota(jnp.int32, (rows, rows), 0)
+    across = lax.broadcasted_iota(jnp.int32, (rows, rows), 1)
+    diagonal = jnp.where(across <= down, here[:, free:], NEGATIVE)
+    pieces = [past, diagonal] if free == 0 else [past, here[:, :free], diagonal]
+    scores = jnp.concatenate(pieces, 1)
+    scale = HEAD ** (-0.5)
+    highest = jnp.max(scores, axis=1, keepdims=True)
+    weights = jnp.exp((scores - highest) * scale)
+    total = jnp.sum(weights, axis=1, keepdims=True)
+    rounded = weights.astype(jnp.bfloat16)
+    depth = past_keys.shape[0]
+    summed = jnp.dot(rounded[:, :depth], past_values, preferred_element_type=jnp.float32)
+    summed += jnp.dot(rounded[:, depth:], values, preferred_element_type=jnp.float32)
+    return (summed / total).astype(jnp.bfloat16)
+
+
+def exchange_kernel(
+    seqs, tps, q_ref, k_ref, v_ref, pk_ref, pv_ref, o_ref,
+    hist, hist_tp, hist_all, past_k, past_v, q_buf, k_buf, v_buf, o_buf,
+    tp_send, tp_recv, hist_send, hist_recv, send, recv, o_send, o_recv,
+):
+    me = lax.axis_index("seq")
+    mine = lax.axis_index("tp")
+    rows, wide = q_ref.shape
+    width = wide // seqs
+    heads = width // HEAD
+
+    barrier = pltpu.get_barrier_semaphore()
+    for off in range(1, seqs):
+        pl.semaphore_signal(
+            barrier, inc=1, device_id={"seq": lax.rem(me + off, seqs)},
+            device_id_type=pl.DeviceIdType.MESH,
+        )
+    for off in range(1, tps):
+        pl.semaphore_signal(
+            barrier, inc=1, device_id={"tp": lax.rem(mine + off, tps)},
+            device_id_type=pl.DeviceIdType.MESH,
+        )
+    for part in range(tps):
+        at = slice(part * wide, (part + 1) * wide)
+        both = [pk_ref[:, at].astype(jnp.float32), pv_ref[:, at].astype(jnp.float32)]
+        hist[part] = jnp.concatenate(both, 0).astype(jnp.bfloat16)
+    pl.semaphore_wait(barrier, seqs + tps - 2)
+
+    def columns(number):
+        return pl.ds(pl.multiple_of(number * width, width), width)
+
+    sent = []
+    for off in range(1, tps):
+        other = lax.rem(mine + off, tps)
+        copy = pltpu.make_async_remote_copy(
+            src_ref=hist.at[other], dst_ref=hist_tp.at[mine],
+            send_sem=tp_send.at[off], recv_sem=tp_recv.at[mine],
+            device_id={"tp": other}, device_id_type=pl.DeviceIdType.MESH,
+        )
+        copy.start()
+        sent.append(copy)
+    pltpu.make_async_copy(hist.at[mine], hist_tp.at[mine], tp_recv.at[mine]).start()
+    tensors = ((k_ref, k_buf), (q_ref, q_buf), (v_ref, v_buf))
+    for number, (ref, buf) in enumerate(tensors):
+        for off in range(1, seqs):
+            other = lax.rem(me + off, seqs)
+            copy = pltpu.make_async_remote_copy(
+                src_ref=ref.at[:, columns(other)], dst_ref=buf.at[me],
+                send_sem=send.at[number, off], recv_sem=recv.at[number, me],
+                device_id={"seq": other}, device_id_type=pl.DeviceIdType.MESH,
+            )
+            copy.start()
+            sent.append(copy)
+        pltpu.make_async_copy(ref.at[:, columns(me)], buf.at[me], recv.at[number, me]).start()
+    for part in range(tps):
+        pltpu.make_async_copy(hist_tp.at[part], hist_tp.at[part], tp_recv.at[part]).wait()
+    for off in range(1, seqs):
+        other = lax.rem(me + off, seqs)
+        copy = pltpu.make_async_remote_copy(
+            src_ref=hist_tp.at[:, :, columns(other)], dst_ref=hist_all.at[me],
+            send_sem=hist_send.at[off], recv_sem=hist_recv.at[me],
+            device_id={"seq": other}, device_id_type=pl.DeviceIdType.MESH,
+        )
+        copy.start()
+        sent.append(copy)
+    pltpu.make_async_copy(hist_tp.at[:, :, columns(me)], hist_all.at[me], hist_recv.at[me]).start()
+
+    for source in range(seqs):
+        pltpu.make_async_copy(hist_all.at[source], hist_all.at[source], hist_recv.at[source]).wait()
+        half = hist_all.shape[2] // 2
+        blocks = [hist_all[source, part].astype(jnp.float32) for part in range(tps)]
+        at = slice(source * tps * half, (source + 1) * tps * half)
+        past_k[at, :] = jnp.concatenate([b[:half] for b in blocks], 0).astype(jnp.bfloat16)
+        past_v[at, :] = jnp.concatenate([b[half:] for b in blocks], 0).astype(jnp.bfloat16)
+
+    for block in range(seqs):
+        for number, (ref, buf) in enumerate(tensors):
+            pltpu.make_async_copy(buf.at[block], buf.at[block], recv.at[number, block]).wait()
+        count = (block + 1) * rows
+        for head in range(heads):
+            at = slice(head * HEAD, (head + 1) * HEAD)
+            o_buf[block, :, at] = attend(
+                q_buf[block, :, at],
+                past_k[:, at],
+                past_v[:, at],
+                k_buf[: block + 1, :, at].reshape(count, HEAD),
+                v_buf[: block + 1, :, at].reshape(count, HEAD),
+            )
+
+        @pl.when(me != block)
+        def _():
+            pltpu.make_async_remote_copy(
+                src_ref=o_buf.at[block], dst_ref=o_ref.at[:, columns(me)],
+                send_sem=o_send.at[block], recv_sem=o_recv.at[me],
+                device_id={"seq": block}, device_id_type=pl.DeviceIdType.MESH,
+            ).start()
+
+        @pl.when(me == block)
+        def _():
+            pltpu.make_async_copy(o_buf.at[block], o_ref.at[:, columns(me)], o_recv.at[me]).start()
+
+    for copy in sent:
+        copy.wait_send()
+    for block in range(seqs):
+        spot = o_ref.at[:, block * width : (block + 1) * width]
+        pltpu.make_async_copy(spot, spot, o_recv.at[block]).wait()
+
+        @pl.when(me != block)
+        def _():
+            pltpu.make_async_copy(o_buf.at[block], o_buf.at[block], o_send.at[block]).wait()
+
+
+def local_kernel(seqs, tps, att_query, att_key, att_value, past_key, past_value):
+    rows, wide = att_query.shape
+    width = wide // seqs
+    past_rows = past_key.shape[0]
+    depth = past_rows * seqs * tps
+    anywhere = pl.BlockSpec(memory_space=pl.ANY)
+    near = pl.BlockSpec(memory_space=pltpu.VMEM)
+    bf16 = jnp.bfloat16
+    dma = pltpu.SemaphoreType.DMA
+    return pl.pallas_call(
+        functools.partial(exchange_kernel, seqs, tps),
+        out_shape=jax.ShapeDtypeStruct((rows, wide), bf16),
+        in_specs=[anywhere, anywhere, anywhere, near, near],
+        out_specs=near,
+        scratch_shapes=[
+            pltpu.VMEM((tps, 2 * past_rows, wide), bf16),
+            pltpu.VMEM((tps, 2 * past_rows, wide), bf16),
+            pltpu.VMEM((seqs, tps, 2 * past_rows, width), bf16),
+            pltpu.VMEM((depth, width), bf16),
+            pltpu.VMEM((depth, width), bf16),
+            pltpu.VMEM((seqs, rows, width), bf16),
+            pltpu.VMEM((seqs, rows, width), bf16),
+            pltpu.VMEM((seqs, rows, width), bf16),
+            pltpu.VMEM((seqs, rows, width), bf16),
+            dma((tps,)),
+            dma((tps,)),
+            dma((seqs,)),
+            dma((seqs,)),
+            dma((3, seqs)),
+            dma((3, seqs)),
+            dma((seqs,)),
+            dma((seqs,)),
+        ],
+        compiler_params=pltpu.CompilerParams(
+            collective_id=0, has_side_effects=True, vmem_limit_bytes=40 * 2**20
+        ),
+    )(att_query, att_key, att_value, past_key, past_value)
+
+
+def local(att_query, att_key, att_value, past_key, past_value):
+    seqs, tps = lax.axis_size("seq"), lax.axis_size("tp")
+    rows, wide = att_query.shape
+    fits = wide % (seqs * HEAD) == 0 and wide * tps == past_key.shape[1]
+    if fits and past_key.shape[0] == 8 and rows % 16 == 0 and rows <= 256 and seqs <= 8:
+        return local_kernel(seqs, tps, att_query, att_key, att_value, past_key, past_value)
+    return local_xla(att_query, att_key, att_value, past_key, past_value)
+
+
 def solution(mesh):
     placed = (
         P("seq", "tp"),

time: 127 us -> 67.3 us (0.53)
  the two profiles are of different devices: /device:TPU:0 before, /device:TPU:30 now
where the time goes in v1:
time: 67.3 us; the launch traced here: 67 us
  Pallas kernels  61.2 us (91%)
  local copies, waits for them, and re-layouts  5.73 us (9%)
    pallas_call x1, Pallas kernels, local_kernel(): pl.pallas_call(functools.partial(exchange_kernel, seqs, tps), out_shape=j...  61.2 us
    unnamed x11, local copies, waits for them, and re-layouts  5.73 us

profile of v1, /device:TPU:30, one launch (start us, length us, event | category | flops | bytes accessed | tf_op | source)
XLA Modules:
  0.0 67.0 jit_solution(10701733638687483609)
XLA Ops:
  0.0 0.0 copy-start
  0.0 1.0 %copy-done = bf16[128,2048]{1,0:T(8,128)(2,1)S(1)} copy-done((bf16[128,2048]{1,0:T(8,128)(2,1)S(1)}, bf16[128,2048]{1,0:T(8,128)(2,1)}, u32[]{:S(2)}) %copy-start) | copy-done | bytes 524312
  1.0 0.0 copy-start.1
  1.0 1.0 %copy-done.1 = bf16[128,2048]{1,0:T(8,128)(2,1)S(1)} copy-done((bf16[128,2048]{1,0:T(8,128)(2,1)S(1)}, bf16[128,2048]{1,0:T(8,128)(2,1)}, u32[]{:S(2)}) %copy-start.1) | copy-done | bytes 524312
  2.1 0.0 copy-start.2
  2.1 1.0 %copy-done.2 = bf16[128,2048]{1,0:T(8,128)(2,1)S(1)} copy-done((bf16[128,2048]{1,0:T(8,128)(2,1)S(1)}, bf16[128,2048]{1,0:T(8,128)(2,1)}, u32[]{:S(2)}) %copy-start.2) | copy-done | bytes 524312
  3.1 0.0 copy-start.3
  3.1 0.9 %copy-done.3 = bf16[8,8192]{1,0:T(8,128)(2,1)S(1)} copy-done((bf16[8,8192]{1,0:T(8,128)(2,1)S(1)}, bf16[8,8192]{1,0:T(8,128)(2,1)}, u32[]{:S(2)}) %copy-start.3) | copy-done | bytes 131096
  4.0 0.0 copy-start.4
  4.0 0.9 %copy-done.4 = bf16[8,8192]{1,0:T(8,128)(2,1)S(1)} copy-done((bf16[8,8192]{1,0:T(8,128)(2,1)S(1)}, bf16[8,8192]{1,0:T(8,128)(2,1)}, u32[]{:S(2)}) %copy-start.4) | copy-done | bytes 131096
  4.9 61.2 %shard_map.55 = bf16[128,2048]{1,0:T(8,128)(2,1)S(1)} custom-call(bf16[128,2048]{1,0:T(8,128)(2,1)S(1)} %copy-done, bf16[128,2048]{1,0:T(8,128)(2,1)S(1)} %copy-done.1, bf16[128,2048]{1,0:T(8,128)(2,1)S(1)} %copy-done.2, bf16[8,8192]{1,0:T(8,128)(2,1)S(1)} %copy-done.3, bf16[8,8192]{1,0:T(8,128)(2,1)S(1)} %copy-done.4), custom_call_target="tpu_custom_call" | custom-call | tf_op jit(solution)/shard_map/pallas_call | solution.py:280
  66.2 0.8 %copy.7 = bf16[128,2048]{1,0:T(8,128)(2,1)} copy(bf16[128,2048]{1,0:T(8,128)(2,1)S(1)} %shard_map.55) | data formatting | bytes 1048576
Async XLA Ops:
  0.0 1.0 %copy-start = (bf16[128,2048]{1,0:T(8,128)(2,1)S(1)}, bf16[128,2048]{1,0:T(8,128)(2,1)}, u32[]{:S(2)}) copy-start(bf16[128,2048]{1,0:T(8,128)(2,1)} %q_ref.1) | copy-start | bytes 1572868
  1.0 1.0 %copy-start.1 = (bf16[128,2048]{1,0:T(8,128)(2,1)S(1)}, bf16[128,2048]{1,0:T(8,128)(2,1)}, u32[]{:S(2)}) copy-start(bf16[128,2048]{1,0:T(8,128)(2,1)} %k_ref.1) | copy-start | bytes 1572868
  2.1 1.0 %copy-start.2 = (bf16[128,2048]{1,0:T(8,128)(2,1)S(1)}, bf16[128,2048]{1,0:T(8,128)(2,1)}, u32[]{:S(2)}) copy-start(bf16[128,2048]{1,0:T(8,128)(2,1)} %v_ref.1) | copy-start | bytes 1572868
  3.1 0.9 %copy-start.3 = (bf16[8,8192]{1,0:T(8,128)(2,1)S(1)}, bf16[8,8192]{1,0:T(8,128)(2,1)}, u32[]{:S(2)}) copy-start(bf16[8,8192]{1,0:T(8,128)(2,1)} %pk_ref.1) | copy-start | bytes 393220
  4.0 0.9 %copy-start.4 = (bf16[8,8192]{1,0:T(8,128)(2,1)S(1)}, bf16[8,8192]{1,0:T(8,128)(2,1)}, u32[]{:S(2)}) copy-start(bf16[8,8192]{1,0:T(8,128)(2,1)} %pv_ref.1) | copy-start | bytes 393220

commit v2 on v0

--- a/solution.py
+++ b/solution.py
@@ -1,6 +1,10 @@
+import functools
+
 import jax
 import jax.numpy as jnp
 from jax import lax
+from jax.experimental import pallas as pl
+from jax.experimental.pallas import tpu as pltpu
 from jax.sharding import PartitionSpec as P
 
 HEAD = 128
@@ -53,7 +57,7 @@
     )
 
 
-def local(att_query, att_key, att_value, past_key, past_value):
+def local_xla(att_query, att_key, att_value, past_key, past_value):
     seq_count = lax.axis_size("seq")
     position = lax.axis_index("seq")
     past_keys, past_values = (
@@ -130,6 +134,470 @@
     return summed.reshape(rows, heads_here * HEAD).astype(jnp.bfloat16)
 
 
+SCALE = HEAD ** (-0.5)
+CHUNKS = 4
+
+
+def partial(query, pieces, diagonal):
+    contract = (((1,), (1,)), ((), ()))
+    found = [
+        lax.dot_general(keys, query, contract, preferred_element_type=jnp.float32)
+        for keys, values in pieces
+    ]
+    if diagonal:
+        shape = found[-1].shape
+        key_at = lax.broadcasted_iota(jnp.int32, shape, 0)
+        query_at = lax.broadcasted_iota(jnp.int32, shape, 1)
+        found[-1] = jnp.where(key_at <= query_at, found[-1], NEGATIVE)
+    highest = functools.reduce(
+        jnp.maximum, [jnp.max(scores, axis=0, keepdims=True) for scores in found]
+    )
+    total = jnp.zeros_like(highest)
+    summed = jnp.zeros((HEAD, query.shape[0]), jnp.float32)
+    for scores, (keys, values) in zip(found, pieces):
+        weights = jnp.exp((scores - highest) * SCALE)
+        total += jnp.sum(weights, axis=0, keepdims=True)
+        summed += lax.dot_general(
+            values, weights.astype(jnp.bfloat16), (((0,), (0,)), ((), ())),
+            preferred_element_type=jnp.float32,
+        )
+    return summed / total, highest * SCALE + jnp.log(total)
+
+
+def merge(parts):
+    top = functools.reduce(jnp.maximum, [level for rows, level in parts])
+    shares = [jnp.exp(level - top) for rows, level in parts]
+    out = sum(rows * share for (rows, level), share in zip(parts, shares))
+    return out / sum(shares)
+
+
+def wait(ref, sem):
+    pltpu.make_async_copy(ref, ref, sem).wait()
+
+
+def chain_kernel(
+    tps, q_ref, k_ref, v_ref, pk_ref, pv_ref, o_ref,
+    hist, hist_tp, slab, past_k, past_v, own, far_q, far_kv, got_o, got_l, give_o, give_l,
+    keep_o, keep_l, o_buf,
+    tp_send, tp_recv, hy_send, hy_recv, hz_send, hz_recv, own_send, own_recv,
+    far_send, far_q_recv, far_kv_recv, go_send, go_recv, gl_send, gl_recv, fin_send, fin_recv,
+):
+    seqs, zs = 8, 4
+    me = lax.axis_index("seq")
+    mine = lax.axis_index("tp")
+    z, y = me // 2, lax.rem(me, 2)
+    peer = z * 2 + 1 - y
+    rows, wide = q_ref.shape
+    half = wide // 2
+    width = half // CHUNKS
+    heads = width // HEAD
+    mesh_id = pl.DeviceIdType.MESH
+
+    barrier = pltpu.get_barrier_semaphore()
+    for off in range(1, seqs):
+        pl.semaphore_signal(
+            barrier, inc=1, device_id={"seq": lax.rem(me + off, seqs)}, device_id_type=mesh_id
+        )
+    for off in range(1, tps):
+        pl.semaphore_signal(
+            barrier, inc=1, device_id={"tp": lax.rem(mine + off, tps)}, device_id_type=mesh_id
+        )
+    for part in range(tps):
+        at = slice(part * wide, (part + 1) * wide)
+        both = [pk_ref[:, at].astype(jnp.float32), pv_ref[:, at].astype(jnp.float32)]
+        hist[part] = jnp.concatenate(both, 0).astype(jnp.bfloat16)
+    pl.semaphore_wait(barrier, seqs + tps - 2)
+
+    def columns(side, chunk):
+        return pl.ds(pl.multiple_of(side * half + chunk * width, width), width)
+
+    def send_to(seq, src, dst, send_sem, recv_sem):
+        pltpu.make_async_remote_copy(
+            src_ref=src, dst_ref=dst, send_sem=send_sem, recv_sem=recv_sem,
+            device_id={"seq": seq}, device_id_type=mesh_id,
+        ).start()
+
+    for off in range(1, tps):
+        other = lax.rem(mine + off, tps)
+        pltpu.make_async_remote_copy(
+            src_ref=hist.at[other], dst_ref=hist_tp.at[mine],
+            send_sem=tp_send.at[off], recv_sem=tp_recv.at[mine],
+            device_id={"tp": other}, device_id_type=mesh_id,
+        ).start()
+    pltpu.make_async_copy(hist.at[mine], hist_tp.at[mine], tp_recv.at[mine]).start()
+
+    def send_far(chunk):
+        @pl.when(z == 0)
+        def _():
+            for side in range(2):
+                for kind, ref in enumerate((k_ref, v_ref)):
+                    send_to(
+                        2 + side, ref.at[:, columns(side, chunk)], far_kv.at[kind, y, chunk],
+                        far_send.at[kind, side, chunk], far_kv_recv.at[kind, y, chunk],
+                    )
+
+        @pl.when(z == 2)
+        def _():
+            for side in range(2):
+                send_to(
+                    2 + side, q_ref.at[:, columns(side, chunk)], far_q.at[0, y, chunk],
+                    far_send.at[0, side, chunk], far_q_recv.at[0, y, chunk],
+                )
+
+        @pl.when(z == 3)
+        def _():
+            for target in range(2):
+                for side in range(2):
+                    send_to(
+                        2 + 2 * target + side, q_ref.at[:, columns(side, chunk)],
+                        far_q.at[1, y, chunk],
+                        far_send.at[target, side, chunk], far_q_recv.at[1, y, chunk],
+                    )
+
+    def send_own(chunk):
+        for kind, ref in enumerate((q_ref, k_ref, v_ref)):
+            send_to(
+                peer, ref.at[:, columns(1 - y, chunk)], own.at[kind, y, chunk],
+                own_send.at[kind, chunk], own_recv.at[kind, y, chunk],
+            )
+            pltpu.make_async_copy(
+                ref.at[:, columns(y, chunk)], own.at[kind, y, chunk], own_recv.at[kind, y, chunk]
+            ).start()
+
+    send_far(0)
+    send_own(0)
+    for part in range(tps):
+        wait(hist_tp.at[part], tp_recv.at[part])
+    away = hist_tp.at[:, :, pl.ds(pl.multiple_of((1 - y) * half, half), half)]
+    here = hist_tp.at[:, :, pl.ds(pl.multiple_of(y * half, half), half)]
+    send_to(peer, away, slab.at[z, y], hy_send.at[0], hy_recv.at[y])
+    pltpu.make_async_copy(here, slab.at[z, y], hy_recv.at[y]).start()
+    send_far(1)
+    for side in range(2):
+        wait(slab.at[z, side], hy_recv.at[side])
+
+    def pass_slab(number, target):
+        send_to(
+            target * 2 + y, slab.at[number], slab.at[number], hz_send.at[number], hz_recv.at[number]
+        )
+
+    for origin in range(zs):
+        pl.when(z == origin)(
+            functools.partial(pass_slab, origin, 1 if origin == 0 else origin - 1)
+        )
+
+    @pl.when(z == 2)
+    def _():
+        wait(slab.at[3], hz_recv.at[3])
+        pass_slab(3, 1)
+
+    for chunk in range(1, CHUNKS):
+        if chunk > 1:
+            send_far(chunk)
+        send_own(chunk)
+
+    def settle(number):
+        past_rows = slab.shape[3] // 2
+        count = 2 * tps * past_rows
+        at = slice(number * count, (number + 1) * count)
+        for chunk in range(CHUNKS):
+            cut = slice(chunk * width, (chunk + 1) * width)
+            blocks = [
+                slab[number, side, part, :, cut].astype(jnp.float32)
+                for side in range(2)
+                for part in range(tps)
+            ]
+            past_k[chunk, at] = jnp.concatenate([b[:past_rows] for b in blocks], 0).astype(jnp.bfloat16)
+            past_v[chunk, at] = jnp.concatenate([b[past_rows:] for b in blocks], 0).astype(jnp.bfloat16)
+
+    def lanes(head):
+        return slice(head * HEAD, (head + 1) * HEAD)
+
+    def own_of(kind, chunk, head):
+        return own[kind, :, chunk, :, lanes(head)].reshape(2 * rows, HEAD)
+
+    def far_q_of(slot, chunk, head):
+        return far_q[slot, :, chunk, :, lanes(head)].reshape(2 * rows, HEAD)
+
+    def near_pair(chunk, head):
+        return own_of(1, chunk, head), own_of(2, chunk, head)
+
+    def far_pair(chunk, head):
+        return tuple(
+            far_kv[kind, :, chunk, :, lanes(head)].reshape(2 * rows, HEAD) for kind in range(2)
+        )
+
+    def past_pair(chunk, head, first, last):
+        at = slice(first * past_k.shape[1] // zs, last * past_k.shape[1] // zs)
+        return past_k[chunk, at, lanes(head)], past_v[chunk, at, lanes(head)]
+
+    def wait_own(chunk):
+        for kind in range(3):
+            for side in range(2):
+                wait(own.at[kind, side, chunk], own_recv.at[kind, side, chunk])
+
+    def wait_far_q(slot, chunk):
+        for side in range(2):
+            wait(far_q.at[slot, side, chunk], far_q_recv.at[slot, side, chunk])
+
+    def give(slot, target, source, chunk):
+        send_to(
+            target * 2 + y, give_o.at[slot, chunk], got_o.at[source, chunk],
+            go_send.at[slot, chunk], go_recv.at[source, chunk],
+        )
+        send_to(
+            target * 2 + y, give_l.at[slot, chunk], got_l.at[source, chunk],
+            gl_send.at[slot, chunk], gl_recv.at[source, chunk],
+        )
+
+    def put_part(slot, chunk, head, part):
+        give_o[slot, chunk, head] = part[0].astype(jnp.bfloat16)
+        give_l[slot, chunk, head] = jnp.broadcast_to(part[1], give_l.shape[3:])
+
+    def put_result(chunk, head, result):
+        flat = jnp.transpose(result).astype(jnp.bfloat16)
+        for side in range(2):
+            o_buf[chunk, side, :, lanes(head)] = flat[side * rows : (side + 1) * rows]
+
+    def finish_chunk(chunk):
+        spot = o_ref.at[:, columns(y, chunk)]
+        send_to(peer, o_buf.at[chunk, 1 - y], spot, fin_send.at[chunk], fin_recv.at[y, chunk])
+        pltpu.make_async_copy(o_buf.at[chunk, y], spot, fin_recv.at[y, chunk]).start()
+
+    def each_chunk(first, body):
+        def step(chunk, unused):
+            body(chunk)
+            return unused
+
+        lax.fori_loop(first, CHUNKS, step, 0)
+
+    def wait_slabs(numbers):
+        for number in numbers:
+            wait(slab.at[number], hz_recv.at[number])
+
+    def sent_slabs(numbers):
+        for number in numbers:
+            wait(slab.at[number], hz_send.at[number])
+
+    def sent_far(targets, sides):
+        def body(chunk):
+            for target in range(targets):
+                for side in range(sides):
+                    wait(far_q.at[0, 0, 0], far_send.at[target, side, chunk])
+
+        each_chunk(0, body)
+
+    def sent_parts(slots):
+        def body(chunk):
+            for slot in slots:
+                wait(give_o.at[slot, chunk], go_send.at[slot, chunk])
+                wait(give_l.at[slot, chunk], gl_send.at[slot, chunk])
+
+        each_chunk(0, body)
+
+    @pl.when(z == 0)
+    def _():
+        wait_slabs((1, 2, 3))
+        for number in range(zs):
+            settle(number)
+
+        def body(chunk):
+            wait_own(chunk)
+            for head in range(heads):
+                pieces = [past_pair(chunk, head, 0, zs), near_pair(chunk, head)]
+                put_result(chunk, head, partial(own_of(0, chunk, head), pieces, True)[0])
+            finish_chunk(chunk)
+
+        each_chunk(0, body)
+        sent_slabs((0,))
+        sent_far(2, 2)
+
+    @pl.when(z == 1)
+    def _():
+        wait_slabs((0,))
+        settle(0)
+        settle(1)
+
+        def far_part(chunk):
+            wait_own(chunk)
+            for kind in range(2):
+                for side in range(2):
+                    wait(far_kv.at[kind, side, chunk], far_kv_recv.at[kind, side, chunk])
+            for slot in (1, 0):
+                wait_far_q(slot, chunk)
+                for head in range(heads):
+                    pieces = [
+                        past_pair(chunk, head, 0, 2), far_pair(chunk, head), near_pair(chunk, head)
+                    ]
+                    put_part(slot, chunk, head, partial(far_q_of(slot, chunk, head), pieces, False))
+                give(slot, 2 + slot, 0, chunk)
+
+        def own_part(chunk):
+            for head in range(heads):
+                pieces = [
+                    past_pair(chunk, head, 0, zs), far_pair(chunk, head), near_pair(chunk, head)
+                ]
+                put_result(chunk, head, partial(own_of(0, chunk, head), pieces, True)[0])
+            finish_chunk(chunk)
+
+        def body(chunk):
+            far_part(chunk)
+
+            @pl.when(chunk == 0)
+            def _():
+                for number in (2, 3):
+                    wait_slabs((number,))
+                    pass_slab(number, 0)
+                    settle(number)
+
+            own_part(chunk)
+
+        each_chunk(0, body)
+        sent_slabs((1, 2, 3))
+        sent_parts((0, 1))
+
+    def keep(chunk, head, part):
+        keep_o[chunk, head] = part[0]
+        keep_l[chunk, head] = jnp.broadcast_to(part[1], keep_l.shape[2:])
+
+    def combine(sources):
+        def body(chunk):
+            for source in sources:
+                wait(got_o.at[source, chunk], go_recv.at[source, chunk])
+                wait(got_l.at[source, chunk], gl_recv.at[source, chunk])
+            for head in range(heads):
+                parts = [(keep_o[chunk, head], keep_l[chunk, head, :1])]
+                for source in sources:
+                    parts.append(
+                        (
+                            got_o[source, chunk, head].astype(jnp.float32),
+                            got_l[source, chunk, head, :1],
+                        )
+                    )
+                put_result(chunk, head, merge(parts))
+            finish_chunk(chunk)
+
+        each_chunk(0, body)
+
+    @pl.when(z == 2)
+    def _():
+        settle(2)
+        settle(3)
+
+        def body(chunk):
+            wait_own(chunk)
+            wait_far_q(1, chunk)
+            for head in range(heads):
+                pieces = [past_pair(chunk, head, 2, zs), near_pair(chunk, head)]
+                put_part(1, chunk, head, partial(far_q_of(1, chunk, head), pieces, False))
+            give(1, 3, 1, chunk)
+            for head in range(heads):
+                pieces = [past_pair(chunk, head, 2, zs), near_pair(chunk, head)]
+                keep(chunk, head, partial(own_of(0, chunk, head), pieces, True))
+
+        each_chunk(0, body)
+        combine((0,))
+        sent_slabs((2, 3))
+        sent_far(1, 2)
+        sent_parts((1,))
+
+    @pl.when(z == 3)
+    def _():
+        def body(chunk):
+            wait_own(chunk)
+            for head in range(heads):
+                keep(chunk, head, partial(own_of(0, chunk, head), [near_pair(chunk, head)], True))
+
+        each_chunk(0, body)
+        combine((0, 1))
+        sent_slabs((3,))
+        sent_far(2, 2)
+
+    for off in range(1, tps):
+        wait(hist.at[0], tp_send.at[off])
+    wait(slab.at[0, 0], hy_send.at[0])
+
+    def last(chunk):
+        for kind in range(3):
+            wait(own.at[kind, 0, chunk], own_send.at[kind, chunk])
+        wait(o_buf.at[chunk, 0], fin_send.at[chunk])
+        for side in range(2):
+            wait(o_ref.at[:, columns(side, chunk)], fin_recv.at[side, chunk])
+
+    each_chunk(0, last)
+
+
+def local_chain(tps, att_query, att_key, att_value, past_key, past_value):
+    rows, wide = att_query.shape
+    half = wide // 2
+    width = half // CHUNKS
+    heads = width // HEAD
+    past_rows = past_key.shape[0]
+    depth = past_rows * 8 * tps
+    far = pl.BlockSpec(memory_space=pltpu.HBM)
+    near = pl.BlockSpec(memory_space=pltpu.VMEM)
+    dma = pltpu.SemaphoreType.DMA
+
+    def held(*shape):
+        return pltpu.VMEM(shape, jnp.bfloat16)
+
+    def wider(*shape):
+        return pltpu.VMEM(shape, jnp.float32)
+
+    return pl.pallas_call(
+        functools.partial(chain_kernel, tps),
+        out_shape=jax.ShapeDtypeStruct((rows, wide), jnp.bfloat16),
+        in_specs=[far, far, far, near, near],
+        out_specs=near,
+        scratch_shapes=[
+            held(tps, 2 * past_rows, wide),
+            held(tps, 2 * past_rows, wide),
+            held(4, 2, tps, 2 * past_rows, half),
+            held(CHUNKS, depth, width),
+            held(CHUNKS, depth, width),
+            held(3, 2, CHUNKS, rows, width),
+            held(2, 2, CHUNKS, rows, width),
+            held(2, 2, CHUNKS, rows, width),
+            held(2, CHUNKS, heads, HEAD, 2 * rows),
+            wider(2, CHUNKS, heads, 8, 2 * rows),
+            held(2, CHUNKS, heads, HEAD, 2 * rows),
+            wider(2, CHUNKS, heads, 8, 2 * rows),
+            wider(CHUNKS, heads, HEAD, 2 * rows),
+            wider(CHUNKS, heads, 8, 2 * rows),
+            held(CHUNKS, 2, rows, width),
+            dma((tps,)),
+            dma((tps,)),
+            dma((1,)),
+            dma((2,)),
+            dma((4,)),
+            dma((4,)),
+            dma((3, CHUNKS)),
+            dma((3, 2, CHUNKS)),
+            dma((2, 2, CHUNKS)),
+            dma((2, 2, CHUNKS)),
+            dma((2, 2, CHUNKS)),
+            dma((2, CHUNKS)),
+            dma((2, CHUNKS)),
+            dma((2, CHUNKS)),
+            dma((2, CHUNKS)),
+            dma((CHUNKS,)),
+            dma((2, CHUNKS)),
+        ],
+        compiler_params=pltpu.CompilerParams(
+            collective_id=0, has_side_effects=True, vmem_limit_bytes=56 * 2**20
+        ),
+    )(att_query, att_key, att_value, past_key, past_value)
+
+
+def local(att_query, att_key, att_value, past_key, past_value):
+    seqs, tps = lax.axis_size("seq"), lax.axis_size("tp")
+    rows, wide = att_query.shape
+    fits = wide % (2 * CHUNKS * HEAD) == 0 and wide * tps == past_key.shape[1]
+    if seqs == 8 and fits and past_key.shape[0] == 8 and rows == 128:
+        return local_chain(tps, att_query, att_key, att_value, past_key, past_value)
+    return local_xla(att_query, att_key, att_value, past_key, past_value)
+
+
 def solution(mesh):
     placed = (
         P("seq", "tp"),

time: 127 us -> 70.3 us (0.55)
  the two profiles are of different devices: /device:TPU:0 before, /device:TPU:18 now
where the time goes in v2:
time: 70.3 us; the launch traced here: 70.1 us
  Pallas kernels  68.2 us (97%)
  local copies, waits for them, and re-layouts  1.88 us (3%)
    pallas_call x1, Pallas kernels, local_chain(): pl.pallas_call(functools.partial(chain_kernel, tps), out_shape=jax.ShapeD...  68.2 us
    unnamed x1, local copies, waits for them, and re-layouts  1.88 us

profile of v2, /device:TPU:18, one launch (start us, length us, event | category | flops | bytes accessed | tf_op | source)
XLA Modules:
  0.0 70.1 jit_solution(1833091944598393299)
XLA Ops:
  0.0 68.2 %shard_map.55 = bf16[128,2048]{1,0:T(8,128)(2,1)} custom-call(bf16[128,2048]{1,0:T(8,128)(2,1)} %q_ref.1, bf16[128,2048]{1,0:T(8,128)(2,1)} %k_ref.1, bf16[128,2048]{1,0:T(8,128)(2,1)} %v_ref.1, bf16[8,8192]{1,0:T(8,128)(2,1)} %pk_ref.1, bf16[8,8192]{1,0:T(8,128)(2,1)} %pv_ref.1), custom_call_target="tpu_custom_call" | custom-call | tf_op jit(solution)/shard_map/pallas_call | solution.py:547
  68.2 1.9 %copy.7 = bf16[128,2048]{1,0:T(8,128)(2,1)} copy(bf16[128,2048]{1,0:T(8,128)(2,1)} %shard_map.55) | data formatting | bytes 1048576

commit v3 on v2

--- a/solution.py
+++ b/solution.py
@@ -136,6 +136,7 @@
 
 SCALE = HEAD ** (-0.5)
 CHUNKS = 4
+AHEAD = 2
 
 
 def partial(query, pieces, diagonal):
@@ -272,7 +273,9 @@
     here = hist_tp.at[:, :, pl.ds(pl.multiple_of(y * half, half), half)]
     send_to(peer, away, slab.at[z, y], hy_send.at[0], hy_recv.at[y])
     pltpu.make_async_copy(here, slab.at[z, y], hy_recv.at[y]).start()
-    send_far(1)
+    for chunk in range(1, AHEAD):
+        send_far(chunk)
+        send_own(chunk)
     for side in range(2):
         wait(slab.at[z, side], hy_recv.at[side])
 
@@ -291,10 +294,21 @@
         wait(slab.at[3], hz_recv.at[3])
         pass_slab(3, 1)
 
-    for chunk in range(1, CHUNKS):
-        if chunk > 1:
-            send_far(chunk)
-        send_own(chunk)
+    def advance(chunk):
+        for kind in range(3):
+            wait(own.at[kind, 0, chunk], own_send.at[kind, chunk])
+        for origin, targets in ((0, 2), (2, 1), (3, 2)):
+
+            @pl.when(z == origin)
+            def _():
+                for target in range(targets):
+                    for side in range(2):
+                        wait(far_q.at[0, 0, 0], far_send.at[target, side, chunk])
+
+        @pl.when(chunk + AHEAD < CHUNKS)
+        def _():
+            send_far(chunk + AHEAD)
+            send_own(chunk + AHEAD)
 
     def settle(number):
         past_rows = slab.shape[3] // 2
@@ -379,14 +393,6 @@
         for number in numbers:
             wait(slab.at[number], hz_send.at[number])
 
-    def sent_far(targets, sides):
-        def body(chunk):
-            for target in range(targets):
-                for side in range(sides):
-                    wait(far_q.at[0, 0, 0], far_send.at[target, side, chunk])
-
-        each_chunk(0, body)
-
     def sent_parts(slots):
         def body(chunk):
             for slot in slots:
@@ -397,6 +403,7 @@
 
     @pl.when(z == 0)
     def _():
+        each_chunk(0, advance)
         wait_slabs((1, 2, 3))
         for number in range(zs):
             settle(number)
@@ -410,7 +417,6 @@
 
         each_chunk(0, body)
         sent_slabs((0,))
-        sent_far(2, 2)
 
     @pl.when(z == 1)
     def _():
@@ -419,6 +425,7 @@
         settle(1)
 
         def far_part(chunk):
+            advance(chunk)
             wait_own(chunk)
             for kind in range(2):
                 for side in range(2):
@@ -485,6 +492,7 @@
         settle(3)
 
         def body(chunk):
+            advance(chunk)
             wait_own(chunk)
             wait_far_q(1, chunk)
             for head in range(heads):
@@ -498,12 +506,12 @@
         each_chunk(0, body)
         combine((0,))
         sent_slabs((2, 3))
-        sent_far(1, 2)
         sent_parts((1,))
 
     @pl.when(z == 3)
     def _():
         def body(chunk):
+            advance(chunk)
             wait_own(chunk)
             for head in range(heads):
                 keep(chunk, head, partial(own_of(0, chunk, head), [near_pair(chunk, head)], True))
@@ -511,15 +519,12 @@
         each_chunk(0, body)
         combine((0, 1))
         sent_slabs((3,))
-        sent_far(2, 2)
 
     for off in range(1, tps):
         wait(hist.at[0], tp_send.at[off])
     wait(slab.at[0, 0], hy_send.at[0])
 
     def last(chunk):
-        for kind in range(3):
-            wait(own.at[kind, 0, chunk], own_send.at[kind, chunk])
         wait(o_buf.at[chunk, 0], fin_send.at[chunk])
         for side in range(2):
             wait(o_ref.at[:, columns(side, chunk)], fin_recv.at[side, chunk])
@@ -584,7 +589,7 @@
             dma((2, CHUNKS)),
         ],
         compiler_params=pltpu.CompilerParams(
-            collective_id=0, has_side_effects=True, vmem_limit_bytes=56 * 2**20
+            collective_id=0, has_side_effects=True, vmem_limit_bytes=40 * 2**20
         ),
     )(att_query, att_key, att_value, past_key, past_value)
 

time: 70.3 us -> 69.9 us (level)
  Pallas kernels: 68.2 us -> 63.3 us
  local copies, waits for them, and re-layouts: 1.88 us -> 5.73 us
    pallas_call x1, Pallas kernels: 68.2 us -> 63.3 us  [local_chain(): pl.pallas_call(functools.partial(chain_kernel, tps), out_shape=jax.ShapeD...]
    unnamed x1 -> x11, local copies, waits for them, and re-layouts: 1.88 us -> 5.73 us
where the time goes in v3:
time: 69.9 us; the launch traced here: 69.1 us
  Pallas kernels  63.3 us (91%)
  local copies, waits for them, and re-layouts  5.73 us (8%)
    pallas_call x1, Pallas kernels, local_chain(): pl.pallas_call(functools.partial(chain_kernel, tps), out_shape=jax.ShapeD...  63.3 us
    unnamed x11, local copies, waits for them, and re-layouts  5.73 us

profile of v3, /device:TPU:18, one launch (start us, length us, event | category | flops | bytes accessed | tf_op | source)
XLA Modules:
  0.0 69.1 jit_solution(950689667090824095)
XLA Ops:
  0.0 0.0 copy-start
  0.0 1.0 %copy-done = bf16[128,2048]{1,0:T(8,128)(2,1)S(1)} copy-done((bf16[128,2048]{1,0:T(8,128)(2,1)S(1)}, bf16[128,2048]{1,0:T(8,128)(2,1)}, u32[]{:S(2)}) %copy-start) | copy-done | bytes 524312
  1.0 0.0 copy-start.1
  1.0 1.0 %copy-done.1 = bf16[128,2048]{1,0:T(8,128)(2,1)S(1)} copy-done((bf16[128,2048]{1,0:T(8,128)(2,1)S(1)}, bf16[128,2048]{1,0:T(8,128)(2,1)}, u32[]{:S(2)}) %copy-start.1) | copy-done | bytes 524312
  2.1 0.0 copy-start.2
  2.1 1.0 %copy-done.2 = bf16[128,2048]{1,0:T(8,128)(2,1)S(1)} copy-done((bf16[128,2048]{1,0:T(8,128)(2,1)S(1)}, bf16[128,2048]{1,0:T(8,128)(2,1)}, u32[]{:S(2)}) %copy-start.2) | copy-done | bytes 524312
  3.1 0.0 copy-start.3
  3.1 0.9 %copy-done.3 = bf16[8,8192]{1,0:T(8,128)(2,1)S(1)} copy-done((bf16[8,8192]{1,0:T(8,128)(2,1)S(1)}, bf16[8,8192]{1,0:T(8,128)(2,1)}, u32[]{:S(2)}) %copy-start.3) | copy-done | bytes 131096
  4.0 0.0 copy-start.4
  4.0 0.9 %copy-done.4 = bf16[8,8192]{1,0:T(8,128)(2,1)S(1)} copy-done((bf16[8,8192]{1,0:T(8,128)(2,1)S(1)}, bf16[8,8192]{1,0:T(8,128)(2,1)}, u32[]{:S(2)}) %copy-start.4) | copy-done | bytes 131096
  4.9 63.3 %shard_map.55 = bf16[128,2048]{1,0:T(8,128)(2,1)S(1)} custom-call(bf16[128,2048]{1,0:T(8,128)(2,1)S(1)} %copy-done, bf16[128,2048]{1,0:T(8,128)(2,1)S(1)} %copy-done.1, bf16[128,2048]{1,0:T(8,128)(2,1)S(1)} %copy-done.2, bf16[8,8192]{1,0:T(8,128)(2,1)S(1)} %copy-done.3, bf16[8,8192]{1,0:T(8,128)(2,1)S(1)} %copy-done.4), custom_call_target="tpu_custom_call" | custom-call | tf_op jit(solution)/shard_map/pallas_call | solution.py:552
  68.3 0.8 %copy.7 = bf16[128,2048]{1,0:T(8,128)(2,1)} copy(bf16[128,2048]{1,0:T(8,128)(2,1)S(1)} %shard_map.55) | data formatting | bytes 1048576
Async XLA Ops:
  0.0 1.0 %copy-start = (bf16[128,2048]{1,0:T(8,128)(2,1)S(1)}, bf16[128,2048]{1,0:T(8,128)(2,1)}, u32[]{:S(2)}) copy-start(bf16[128,2048]{1,0:T(8,128)(2,1)} %q_ref.1) | copy-start | bytes 1572868
  1.0 1.0 %copy-start.1 = (bf16[128,2048]{1,0:T(8,128)(2,1)S(1)}, bf16[128,2048]{1,0:T(8,128)(2,1)}, u32[]{:S(2)}) copy-start(bf16[128,2048]{1,0:T(8,128)(2,1)} %k_ref.1) | copy-start | bytes 1572868
  2.1 1.0 %copy-start.2 = (bf16[128,2048]{1,0:T(8,128)(2,1)S(1)}, bf16[128,2048]{1,0:T(8,128)(2,1)}, u32[]{:S(2)}) copy-start(bf16[128,2048]{1,0:T(8,128)(2,1)} %v_ref.1) | copy-start | bytes 1572868
  3.1 0.9 %copy-start.3 = (bf16[8,8192]{1,0:T(8,128)(2,1)S(1)}, bf16[8,8192]{1,0:T(8,128)(2,1)}, u32[]{:S(2)}) copy-start(bf16[8,8192]{1,0:T(8,128)(2,1)} %pk_ref.1) | copy-start | bytes 393220
  4.0 0.9 %copy-start.4 = (bf16[8,8192]{1,0:T(8,128)(2,1)S(1)}, bf16[8,8192]{1,0:T(8,128)(2,1)}, u32[]{:S(2)}) copy-start(bf16[8,8192]{1,0:T(8,128)(2,1)} %pv_ref.1) | copy-start | bytes 393220

commit v4 on v2

--- a/solution.py
+++ b/solution.py
@@ -135,7 +135,9 @@
 
 
 SCALE = HEAD ** (-0.5)
+LOG2E = 1.4426950408889634
 CHUNKS = 4
+HEADWAY = 2
 
 
 def partial(query, pieces, diagonal):
@@ -155,7 +157,7 @@
     total = jnp.zeros_like(highest)
     summed = jnp.zeros((HEAD, query.shape[0]), jnp.float32)
     for scores, (keys, values) in zip(found, pieces):
-        weights = jnp.exp((scores - highest) * SCALE)
+        weights = jnp.exp2((scores - highest) * (SCALE * LOG2E))
         total += jnp.sum(weights, axis=0, keepdims=True)
         summed += lax.dot_general(
             values, weights.astype(jnp.bfloat16), (((0,), (0,)), ((), ())),
@@ -226,53 +228,69 @@
         ).start()
     pltpu.make_async_copy(hist.at[mine], hist_tp.at[mine], tp_recv.at[mine]).start()
 
-    def send_far(chunk):
-        @pl.when(z == 0)
-        def _():
-            for side in range(2):
-                for kind, ref in enumerate((k_ref, v_ref)):
-                    send_to(
-                        2 + side, ref.at[:, columns(side, chunk)], far_kv.at[kind, y, chunk],
-                        far_send.at[kind, side, chunk], far_kv_recv.at[kind, y, chunk],
-                    )
-
-        @pl.when(z == 2)
-        def _():
-            for side in range(2):
+    def forward(chunk):
+        for origin, kind, target, buf, slot, sem in (
+            (0, 1, 1, far_kv, 0, far_kv_recv),
+            (0, 2, 1, far_kv, 1, far_kv_recv),
+            (2, 0, 1, far_q, 0, far_q_recv),
+            (3, 0, 1, far_q, 1, far_q_recv),
+            (3, 0, 2, far_q, 1, far_q_recv),
+        ):
+            number = slot if origin == 0 else 2 - target
+
+            @pl.when(z == origin)
+            def _():
                 send_to(
-                    2 + side, q_ref.at[:, columns(side, chunk)], far_q.at[0, y, chunk],
-                    far_send.at[0, side, chunk], far_q_recv.at[0, y, chunk],
+                    target * 2 + y, own.at[kind, :, chunk], buf.at[slot, :, chunk],
+                    far_send.at[number, chunk], sem.at[slot, chunk],
                 )
 
-        @pl.when(z == 3)
-        def _():
-            for target in range(2):
-                for side in range(2):
-                    send_to(
-                        2 + 2 * target + side, q_ref.at[:, columns(side, chunk)],
-                        far_q.at[1, y, chunk],
-                        far_send.at[target, side, chunk], far_q_recv.at[1, y, chunk],
-                    )
-
-    def send_own(chunk):
-        for kind, ref in enumerate((q_ref, k_ref, v_ref)):
-            send_to(
-                peer, ref.at[:, columns(1 - y, chunk)], own.at[kind, y, chunk],
-                own_send.at[kind, chunk], own_recv.at[kind, y, chunk],
-            )
-            pltpu.make_async_copy(
-                ref.at[:, columns(y, chunk)], own.at[kind, y, chunk], own_recv.at[kind, y, chunk]
-            ).start()
-
-    send_far(0)
-    send_own(0)
+    def send_own(kind, chunk):
+        ref = (q_ref, k_ref, v_ref)[kind]
+        send_to(
+            peer, ref.at[:, columns(1 - y, chunk)], own.at[kind, y, chunk],
+            own_send.at[kind, chunk], own_recv.at[kind, y, chunk],
+        )
+        pltpu.make_async_copy(
+            ref.at[:, columns(y, chunk)], own.at[kind, y, chunk], own_recv.at[kind, y, chunk]
+        ).start()
+
+    def wait_own(kind, chunk):
+        for side in range(2):
+            wait(own.at[kind, side, chunk], own_recv.at[kind, side, chunk])
+
+    @pl.when(z >= 2)
+    def _():
+        for chunk in range(CHUNKS):
+            send_own(0, chunk)
+
+    @pl.when(z < 2)
+    def _():
+        for chunk in range(CHUNKS):
+            send_own(1, chunk)
+            send_own(2, chunk)
+
     for part in range(tps):
         wait(hist_tp.at[part], tp_recv.at[part])
     away = hist_tp.at[:, :, pl.ds(pl.multiple_of((1 - y) * half, half), half)]
     here = hist_tp.at[:, :, pl.ds(pl.multiple_of(y * half, half), half)]
     send_to(peer, away, slab.at[z, y], hy_send.at[0], hy_recv.at[y])
     pltpu.make_async_copy(here, slab.at[z, y], hy_recv.at[y]).start()
-    send_far(1)
+
+    @pl.when(z >= 2)
+    def _():
+        for chunk in range(CHUNKS):
+            send_own(1, chunk)
+            send_own(2, chunk)
+        for chunk in range(HEADWAY):
+            wait_own(0, chunk)
+            forward(chunk)
+
+    @pl.when(z < 2)
+    def _():
+        for chunk in range(CHUNKS):
+            send_own(0, chunk)
+
     for side in range(2):
         wait(slab.at[z, side], hy_recv.at[side])
 
@@ -291,10 +309,18 @@
         wait(slab.at[3], hz_recv.at[3])
         pass_slab(3, 1)
 
-    for chunk in range(1, CHUNKS):
-        if chunk > 1:
-            send_far(chunk)
-        send_own(chunk)
+    @pl.when(z >= 2)
+    def _():
+        for chunk in range(HEADWAY, CHUNKS):
+            wait_own(0, chunk)
+            forward(chunk)
+
+    @pl.when(z == 0)
+    def _():
+        for chunk in range(CHUNKS):
+            wait_own(1, chunk)
+            wait_own(2, chunk)
+            forward(chunk)
 
     def settle(number):
         past_rows = slab.shape[3] // 2
@@ -331,14 +357,8 @@
         at = slice(first * past_k.shape[1] // zs, last * past_k.shape[1] // zs)
         return past_k[chunk, at, lanes(head)], past_v[chunk, at, lanes(head)]
 
-    def wait_own(chunk):
-        for kind in range(3):
-            for side in range(2):
-                wait(own.at[kind, side, chunk], own_recv.at[kind, side, chunk])
-
     def wait_far_q(slot, chunk):
-        for side in range(2):
-            wait(far_q.at[slot, side, chunk], far_q_recv.at[slot, side, chunk])
+        wait(far_q.at[slot, :, chunk], far_q_recv.at[slot, chunk])
 
     def give(slot, target, source, chunk):
         send_to(
@@ -378,14 +398,6 @@
     def sent_slabs(numbers):
         for number in numbers:
             wait(slab.at[number], hz_send.at[number])
-
-    def sent_far(targets, sides):
-        def body(chunk):
-            for target in range(targets):
-                for side in range(sides):
-                    wait(far_q.at[0, 0, 0], far_send.at[target, side, chunk])
-
-        each_chunk(0, body)
 
     def sent_parts(slots):
         def body(chunk):
@@ -402,7 +414,7 @@
             settle(number)
 
         def body(chunk):
-            wait_own(chunk)
+            wait_own(0, chunk)
             for head in range(heads):
                 pieces = [past_pair(chunk, head, 0, zs), near_pair(chunk, head)]
                 put_result(chunk, head, partial(own_of(0, chunk, head), pieces, True)[0])
@@ -410,7 +422,6 @@
 
         each_chunk(0, body)
         sent_slabs((0,))
-        sent_far(2, 2)
 
     @pl.when(z == 1)
     def _():
@@ -419,10 +430,10 @@
         settle(1)
 
         def far_part(chunk):
-            wait_own(chunk)
+            for kind in range(3):
+                wait_own(kind, chunk)
             for kind in range(2):
-                for side in range(2):
-                    wait(far_kv.at[kind, side, chunk], far_kv_recv.at[kind, side, chunk])
+                wait(far_kv.at[kind, :, chunk], far_kv_recv.at[kind, chunk])
             for slot in (1, 0):
                 wait_far_q(slot, chunk)
                 for head in range(heads):
@@ -443,16 +454,19 @@
         def body(chunk):
             far_part(chunk)
 
-            @pl.when(chunk == 0)
+            @pl.when(chunk == 1)
             def _():
                 for number in (2, 3):
                     wait_slabs((number,))
                     pass_slab(number, 0)
                     settle(number)
 
-            own_part(chunk)
+            @pl.when(chunk >= 1)
+            def _():
+                own_part(chunk - 1)
 
         each_chunk(0, body)
+        own_part(CHUNKS - 1)
         sent_slabs((1, 2, 3))
         sent_parts((0, 1))
 
@@ -485,7 +499,8 @@
         settle(3)
 
         def body(chunk):
-            wait_own(chunk)
+            wait_own(1, chunk)
+            wait_own(2, chunk)
             wait_far_q(1, chunk)
             for head in range(heads):
                 pieces = [past_pair(chunk, head, 2, zs), near_pair(chunk, head)]
@@ -498,20 +513,19 @@
         each_chunk(0, body)
         combine((0,))
         sent_slabs((2, 3))
-        sent_far(1, 2)
         sent_parts((1,))
 
     @pl.when(z == 3)
     def _():
         def body(chunk):
-            wait_own(chunk)
+            wait_own(1, chunk)
+            wait_own(2, chunk)
             for head in range(heads):
                 keep(chunk, head, partial(own_of(0, chunk, head), [near_pair(chunk, head)], True))
 
         each_chunk(0, body)
         combine((0, 1))
         sent_slabs((3,))
-        sent_far(2, 2)
 
     for off in range(1, tps):
         wait(hist.at[0], tp_send.at[off])
@@ -520,6 +534,13 @@
     def last(chunk):
         for kind in range(3):
             wait(own.at[kind, 0, chunk], own_send.at[kind, chunk])
+        for origin, targets in ((0, 2), (2, 1), (3, 2)):
+
+            @pl.when(z == origin)
+            def _():
+                for target in range(targets):
+                    wait(far_q.at[0, :, chunk], far_send.at[1 - target if origin == 2 else target, chunk])
+
         wait(o_buf.at[chunk, 0], fin_send.at[chunk])
         for side in range(2):
             wait(o_ref.at[:, columns(side, chunk)], fin_recv.at[side, chunk])
@@ -548,7 +569,7 @@
         functools.partial(chain_kernel, tps),
         out_shape=jax.ShapeDtypeStruct((rows, wide), jnp.bfloat16),
         in_specs=[far, far, far, near, near],
-        out_specs=near,
+        out_specs=far,
         scratch_shapes=[
             held(tps, 2 * past_rows, wide),
             held(tps, 2 * past_rows, wide),
@@ -573,9 +594,9 @@
             dma((4,)),
             dma((3, CHUNKS)),
             dma((3, 2, CHUNKS)),
-            dma((2, 2, CHUNKS)),
-            dma((2, 2, CHUNKS)),
-            dma((2, 2, CHUNKS)),
+            dma((2, CHUNKS)),
+            dma((2, CHUNKS)),
+            dma((2, CHUNKS)),
             dma((2, CHUNKS)),
             dma((2, CHUNKS)),
             dma((2, CHUNKS)),

time: 70.3 us -> 66.8 us (0.950)
  Pallas kernels: 68.2 us -> 64.7 us
    pallas_call x1, Pallas kernels: 68.2 us -> 64.7 us  [local_chain(): pl.pallas_call(functools.partial(chain_kernel, tps), out_shape=jax.ShapeD...]
where the time goes in v4:
time: 66.8 us; the launch traced here: 66.6 us
  Pallas kernels  64.7 us (97%)
  local copies, waits for them, and re-layouts  1.88 us (3%)
    pallas_call x1, Pallas kernels, local_chain(): pl.pallas_call(functools.partial(chain_kernel, tps), out_shape=jax.ShapeD...  64.7 us
    unnamed x1, local copies, waits for them, and re-layouts  1.88 us

profile of v4, /device:TPU:18, one launch (start us, length us, event | category | flops | bytes accessed | tf_op | source)
XLA Modules:
  0.0 66.6 jit_solution(13099138062284633405)
XLA Ops:
  0.0 64.7 %shard_map.55 = bf16[128,2048]{1,0:T(8,128)(2,1)} custom-call(bf16[128,2048]{1,0:T(8,128)(2,1)} %q_ref.1, bf16[128,2048]{1,0:T(8,128)(2,1)} %k_ref.1, bf16[128,2048]{1,0:T(8,128)(2,1)} %v_ref.1, bf16[8,8192]{1,0:T(8,128)(2,1)} %pk_ref.1, bf16[8,8192]{1,0:T(8,128)(2,1)} %pv_ref.1), custom_call_target="tpu_custom_call" | custom-call | tf_op jit(solution)/shard_map/pallas_call | solution.py:568
  64.7 1.9 %copy.7 = bf16[128,2048]{1,0:T(8,128)(2,1)} copy(bf16[128,2048]{1,0:T(8,128)(2,1)} %shard_map.55) | data formatting | bytes 1048576

commit v5 on v4

--- a/solution.py
+++ b/solution.py
@@ -137,7 +137,7 @@
 SCALE = HEAD ** (-0.5)
 LOG2E = 1.4426950408889634
 CHUNKS = 4
-HEADWAY = 2
+HEADWAY = 1
 
 
 def partial(query, pieces, diagonal):
@@ -308,6 +308,11 @@
     def _():
         wait(slab.at[3], hz_recv.at[3])
         pass_slab(3, 1)
+        wait(slab.at[2], hz_send.at[2])
+
+    @pl.when(z >= 2)
+    def _():
+        wait(slab.at[3], hz_send.at[3])
 
     @pl.when(z >= 2)
     def _():
@@ -454,19 +459,16 @@
         def body(chunk):
             far_part(chunk)
 
-            @pl.when(chunk == 1)
+            @pl.when(chunk == 0)
             def _():
                 for number in (2, 3):
                     wait_slabs((number,))
                     pass_slab(number, 0)
                     settle(number)
 
-            @pl.when(chunk >= 1)
-            def _():
-                own_part(chunk - 1)
+            own_part(chunk)
 
         each_chunk(0, body)
-        own_part(CHUNKS - 1)
         sent_slabs((1, 2, 3))
         sent_parts((0, 1))
 
@@ -512,7 +514,6 @@
 
         each_chunk(0, body)
         combine((0,))
-        sent_slabs((2, 3))
         sent_parts((1,))
 
     @pl.when(z == 3)
@@ -525,7 +526,6 @@
 
         each_chunk(0, body)
         combine((0, 1))
-        sent_slabs((3,))
 
     for off in range(1, tps):
         wait(hist.at[0], tp_send.at[off])

time: 66.8 us -> 66.8 us (level)
  no operation moved by 1% of the time
where the time goes in v5:
time: 66.8 us; the launch traced here: 66.7 us
  Pallas kernels  64.8 us (97%)
  local copies, waits for them, and re-layouts  1.88 us (3%)
    pallas_call x1, Pallas kernels, local_chain(): pl.pallas_call(functools.partial(chain_kernel, tps), out_shape=jax.ShapeD...  64.8 us
    unnamed x1, local copies, waits for them, and re-layouts  1.88 us

profile of v5, /device:TPU:18, one launch (start us, length us, event | category | flops | bytes accessed | tf_op | source)
XLA Modules:
  0.0 66.7 jit_solution(13576407316388730276)
XLA Ops:
  0.0 64.8 %shard_map.55 = bf16[128,2048]{1,0:T(8,128)(2,1)} custom-call(bf16[128,2048]{1,0:T(8,128)(2,1)} %q_ref.1, bf16[128,2048]{1,0:T(8,128)(2,1)} %k_ref.1, bf16[128,2048]{1,0:T(8,128)(2,1)} %v_ref.1, bf16[8,8192]{1,0:T(8,128)(2,1)} %pk_ref.1, bf16[8,8192]{1,0:T(8,128)(2,1)} %pv_ref.1), custom_call_target="tpu_custom_call" | custom-call | tf_op jit(solution)/shard_map/pallas_call | solution.py:568
  64.8 1.9 %copy.7 = bf16[128,2048]{1,0:T(8,128)(2,1)} copy(bf16[128,2048]{1,0:T(8,128)(2,1)} %shard_map.55) | data formatting | bytes 1048576

commit v6 on v5

--- a/solution.py
+++ b/solution.py
@@ -143,34 +143,41 @@
 def partial(query, pieces, diagonal):
     contract = (((1,), (1,)), ((), ()))
     found = [
-        lax.dot_general(keys, query, contract, preferred_element_type=jnp.float32)
+        lax.dot_general(query, keys, contract, preferred_element_type=jnp.float32)
         for keys, values in pieces
     ]
     if diagonal:
         shape = found[-1].shape
-        key_at = lax.broadcasted_iota(jnp.int32, shape, 0)
-        query_at = lax.broadcasted_iota(jnp.int32, shape, 1)
+        query_at = lax.broadcasted_iota(jnp.int32, shape, 0)
+        key_at = lax.broadcasted_iota(jnp.int32, shape, 1)
         found[-1] = jnp.where(key_at <= query_at, found[-1], NEGATIVE)
-    highest = functools.reduce(
-        jnp.maximum, [jnp.max(scores, axis=0, keepdims=True) for scores in found]
-    )
-    total = jnp.zeros_like(highest)
-    summed = jnp.zeros((HEAD, query.shape[0]), jnp.float32)
-    for scores, (keys, values) in zip(found, pieces):
-        weights = jnp.exp2((scores - highest) * (SCALE * LOG2E))
-        total += jnp.sum(weights, axis=0, keepdims=True)
-        summed += lax.dot_general(
-            values, weights.astype(jnp.bfloat16), (((0,), (0,)), ((), ())),
-            preferred_element_type=jnp.float32,
-        )
+    scores = jnp.concatenate(found, 1)
+    highest = jnp.max(scores, axis=1, keepdims=True)
+    weights = jnp.exp2((scores - highest) * (SCALE * LOG2E))
+    total = jnp.sum(weights, axis=1, keepdims=True)
+    rounded = weights.astype(jnp.bfloat16)
+    summed = jnp.zeros((query.shape[0], HEAD), jnp.float32)
+    start = 0
+    for keys, values in pieces:
+        stop = start + keys.shape[0]
+        summed += jnp.dot(rounded[:, start:stop], values, preferred_element_type=jnp.float32)
+        start = stop
     return summed / total, highest * SCALE + jnp.log(total)
+
+
+def as_row(column):
+    return jnp.transpose(jnp.broadcast_to(column, (column.shape[0], HEAD)))[:8]
+
+
+def as_columns(row):
+    return jnp.transpose(jnp.broadcast_to(row, (HEAD, row.shape[1])))
 
 
 def merge(parts):
     top = functools.reduce(jnp.maximum, [level for rows, level in parts])
     shares = [jnp.exp(level - top) for rows, level in parts]
-    out = sum(rows * share for (rows, level), share in zip(parts, shares))
-    return out / sum(shares)
+    every = sum(shares)
+    return sum(rows * as_columns(share / every) for (rows, level), share in zip(parts, shares))
 
 
 def wait(ref, sem):
@@ -377,10 +384,10 @@
 
     def put_part(slot, chunk, head, part):
         give_o[slot, chunk, head] = part[0].astype(jnp.bfloat16)
-        give_l[slot, chunk, head] = jnp.broadcast_to(part[1], give_l.shape[3:])
+        give_l[slot, chunk, head] = as_row(part[1])
 
     def put_result(chunk, head, result):
-        flat = jnp.transpose(result).astype(jnp.bfloat16)
+        flat = result.astype(jnp.bfloat16)
         for side in range(2):
             o_buf[chunk, side, :, lanes(head)] = flat[side * rows : (side + 1) * rows]
 
@@ -474,7 +481,7 @@
 
     def keep(chunk, head, part):
         keep_o[chunk, head] = part[0]
-        keep_l[chunk, head] = jnp.broadcast_to(part[1], keep_l.shape[2:])
+        keep_l[chunk, head] = as_row(part[1])
 
     def combine(sources):
         def body(chunk):
@@ -579,11 +586,11 @@
             held(3, 2, CHUNKS, rows, width),
             held(2, 2, CHUNKS, rows, width),
             held(2, 2, CHUNKS, rows, width),
-            held(2, CHUNKS, heads, HEAD, 2 * rows),
+            held(2, CHUNKS, heads, 2 * rows, HEAD),
             wider(2, CHUNKS, heads, 8, 2 * rows),
-            held(2, CHUNKS, heads, HEAD, 2 * rows),
+            held(2, CHUNKS, heads, 2 * rows, HEAD),
             wider(2, CHUNKS, heads, 8, 2 * rows),
-            wider(CHUNKS, heads, HEAD, 2 * rows),
+            wider(CHUNKS, heads, 2 * rows, HEAD),
             wider(CHUNKS, heads, 8, 2 * rows),
             held(CHUNKS, 2, rows, width),
             dma((tps,)),

time: 66.8 us -> 67 us (level)
  no operation moved by 1% of the time
where the time goes in v6:
time: 67 us; the launch traced here: 66.8 us
  Pallas kernels  64.9 us (97%)
  local copies, waits for them, and re-layouts  1.88 us (3%)
    pallas_call x1, Pallas kernels, local_chain(): pl.pallas_call(functools.partial(chain_kernel, tps), out_shape=jax.ShapeD...  64.9 us
    unnamed x1, local copies, waits for them, and re-layouts  1.88 us

profile of v6, /device:TPU:18, one launch (start us, length us, event | category | flops | bytes accessed | tf_op | source)
XLA Modules:
  0.0 66.8 jit_solution(8555599407516188939)
XLA Ops:
  0.0 64.9 %shard_map.55 = bf16[128,2048]{1,0:T(8,128)(2,1)} custom-call(bf16[128,2048]{1,0:T(8,128)(2,1)} %q_ref.1, bf16[128,2048]{1,0:T(8,128)(2,1)} %k_ref.1, bf16[128,2048]{1,0:T(8,128)(2,1)} %v_ref.1, bf16[8,8192]{1,0:T(8,128)(2,1)} %pk_ref.1, bf16[8,8192]{1,0:T(8,128)(2,1)} %pv_ref.1), custom_call_target="tpu_custom_call" | custom-call | tf_op jit(solution)/shard_map/pallas_call | solution.py:575
  64.9 1.9 %copy.7 = bf16[128,2048]{1,0:T(8,128)(2,1)} copy(bf16[128,2048]{1,0:T(8,128)(2,1)} %shard_map.55) | data formatting | bytes 1048576

commit v7 on v1

--- a/solution.py
+++ b/solution.py
@@ -8,6 +8,7 @@
 from jax.sharding import PartitionSpec as P
 
 HEAD = 128
+LOG2E = 1.4426950408889634
 
 
 NEGATIVE = -1e30
@@ -147,7 +148,7 @@
     scores = jnp.concatenate(pieces, 1)
     scale = HEAD ** (-0.5)
     highest = jnp.max(scores, axis=1, keepdims=True)
-    weights = jnp.exp((scores - highest) * scale)
+    weights = jnp.exp2((scores - highest) * (scale * LOG2E))
     total = jnp.sum(weights, axis=1, keepdims=True)
     rounded = weights.astype(jnp.bfloat16)
     depth = past_keys.shape[0]
@@ -187,6 +188,7 @@
     def columns(number):
         return pl.ds(pl.multiple_of(number * width, width), width)
 
+    far_first = sorted(range(1, seqs), key=lambda off: abs(off - seqs // 2))
     sent = []
     for off in range(1, tps):
         other = lax.rem(mine + off, tps)
@@ -200,7 +202,7 @@
     pltpu.make_async_copy(hist.at[mine], hist_tp.at[mine], tp_recv.at[mine]).start()
     tensors = ((k_ref, k_buf), (q_ref, q_buf), (v_ref, v_buf))
     for number, (ref, buf) in enumerate(tensors):
-        for off in range(1, seqs):
+        for off in far_first:
             other = lax.rem(me + off, seqs)
             copy = pltpu.make_async_remote_copy(
                 src_ref=ref.at[:, columns(other)], dst_ref=buf.at[me],
@@ -273,7 +275,7 @@
     width = wide // seqs
     past_rows = past_key.shape[0]
     depth = past_rows * seqs * tps
-    anywhere = pl.BlockSpec(memory_space=pl.ANY)
+    anywhere = pl.BlockSpec(memory_space=pltpu.HBM)
     near = pl.BlockSpec(memory_space=pltpu.VMEM)
     bf16 = jnp.bfloat16
     dma = pltpu.SemaphoreType.DMA
@@ -281,7 +283,7 @@
         functools.partial(exchange_kernel, seqs, tps),
         out_shape=jax.ShapeDtypeStruct((rows, wide), bf16),
         in_specs=[anywhere, anywhere, anywhere, near, near],
-        out_specs=near,
+        out_specs=anywhere,
         scratch_shapes=[
             pltpu.VMEM((tps, 2 * past_rows, wide), bf16),
             pltpu.VMEM((tps, 2 * past_rows, wide), bf16),
@@ -302,7 +304,7 @@
             dma((seqs,)),
         ],
         compiler_params=pltpu.CompilerParams(
-            collective_id=0, has_side_effects=True, vmem_limit_bytes=40 * 2**20
+            collective_id=0, has_side_effects=True, vmem_limit_bytes=56 * 2**20
         ),
     )(att_query, att_key, att_value, past_key, past_value)
 

time: 67.3 us -> 64.3 us (0.955)
  local copies, waits for them, and re-layouts: 5.73 us -> 1.88 us
  Pallas kernels: 61.2 us -> 62.2 us
    unnamed x11 -> x1, local copies, waits for them, and re-layouts: 5.73 us -> 1.88 us
    pallas_call x1, Pallas kernels: 61.2 us -> 62.2 us  [local_kernel(): pl.pallas_call(functools.partial(exchange_kernel, seqs, tps), out_shape=j...]
where the time goes in v7:
time: 64.3 us; the launch traced here: 64.1 us
  Pallas kernels  62.2 us (97%)
  local copies, waits for them, and re-layouts  1.88 us (3%)
    pallas_call x1, Pallas kernels, local_kernel(): pl.pallas_call(functools.partial(exchange_kernel, seqs, tps), out_shape=j...  62.2 us
    unnamed x1, local copies, waits for them, and re-layouts  1.88 us

profile of v7, /device:TPU:30, one launch (start us, length us, event | category | flops | bytes accessed | tf_op | source)
XLA Modules:
  0.0 64.1 jit_solution(11890310019708587583)
XLA Ops:
  0.0 62.2 %shard_map.55 = bf16[128,2048]{1,0:T(8,128)(2,1)} custom-call(bf16[128,2048]{1,0:T(8,128)(2,1)} %q_ref.1, bf16[128,2048]{1,0:T(8,128)(2,1)} %k_ref.1, bf16[128,2048]{1,0:T(8,128)(2,1)} %v_ref.1, bf16[8,8192]{1,0:T(8,128)(2,1)} %pk_ref.1, bf16[8,8192]{1,0:T(8,128)(2,1)} %pv_ref.1), custom_call_target="tpu_custom_call" | custom-call | tf_op jit(solution)/shard_map/pallas_call | solution.py:282
  62.2 1.9 %copy.7 = bf16[128,2048]{1,0:T(8,128)(2,1)} copy(bf16[128,2048]{1,0:T(8,128)(2,1)} %shard_map.55) | data formatting | bytes 1048576

commit v8 on v7

--- a/solution.py
+++ b/solution.py
@@ -189,6 +189,9 @@
         return pl.ds(pl.multiple_of(number * width, width), width)
 
     far_first = sorted(range(1, seqs), key=lambda off: abs(off - seqs // 2))
+    def lanes(number, head):
+        return pl.ds(pl.multiple_of(number * width + head * HEAD, HEAD), HEAD)
+
     sent = []
     for off in range(1, tps):
         other = lax.rem(mine + off, tps)
@@ -201,17 +204,23 @@
         sent.append(copy)
     pltpu.make_async_copy(hist.at[mine], hist_tp.at[mine], tp_recv.at[mine]).start()
     tensors = ((k_ref, k_buf), (q_ref, q_buf), (v_ref, v_buf))
-    for number, (ref, buf) in enumerate(tensors):
-        for off in far_first:
-            other = lax.rem(me + off, seqs)
-            copy = pltpu.make_async_remote_copy(
-                src_ref=ref.at[:, columns(other)], dst_ref=buf.at[me],
-                send_sem=send.at[number, off], recv_sem=recv.at[number, me],
-                device_id={"seq": other}, device_id_type=pl.DeviceIdType.MESH,
-            )
-            copy.start()
-            sent.append(copy)
-        pltpu.make_async_copy(ref.at[:, columns(me)], buf.at[me], recv.at[number, me]).start()
+
+    def send_head(head):
+        for number, (ref, buf) in enumerate(tensors):
+            for off in far_first:
+                other = lax.rem(me + off, seqs)
+                copy = pltpu.make_async_remote_copy(
+                    src_ref=ref.at[:, lanes(other, head)], dst_ref=buf.at[head, me],
+                    send_sem=send.at[number, head, off], recv_sem=recv.at[number, head, me],
+                    device_id={"seq": other}, device_id_type=pl.DeviceIdType.MESH,
+                )
+                copy.start()
+                sent.append(copy)
+            pltpu.make_async_copy(
+                ref.at[:, lanes(me, head)], buf.at[head, me], recv.at[number, head, me]
+            ).start()
+
+    send_head(0)
     for part in range(tps):
         pltpu.make_async_copy(hist_tp.at[part], hist_tp.at[part], tp_recv.at[part]).wait()
     for off in range(1, seqs):
@@ -225,6 +234,9 @@
         sent.append(copy)
     pltpu.make_async_copy(hist_tp.at[:, :, columns(me)], hist_all.at[me], hist_recv.at[me]).start()
 
+    for head in range(1, heads):
+        send_head(head)
+
     for source in range(seqs):
         pltpu.make_async_copy(hist_all.at[source], hist_all.at[source], hist_recv.at[source]).wait()
         half = hist_all.shape[2] // 2
@@ -233,41 +245,46 @@
         past_k[at, :] = jnp.concatenate([b[:half] for b in blocks], 0).astype(jnp.bfloat16)
         past_v[at, :] = jnp.concatenate([b[half:] for b in blocks], 0).astype(jnp.bfloat16)
 
-    for block in range(seqs):
-        for number, (ref, buf) in enumerate(tensors):
-            pltpu.make_async_copy(buf.at[block], buf.at[block], recv.at[number, block]).wait()
-        count = (block + 1) * rows
-        for head in range(heads):
-            at = slice(head * HEAD, (head + 1) * HEAD)
-            o_buf[block, :, at] = attend(
-                q_buf[block, :, at],
+    for head in range(heads):
+        at = slice(head * HEAD, (head + 1) * HEAD)
+        for block in range(seqs):
+            for number, (ref, buf) in enumerate(tensors):
+                spot = buf.at[head, block]
+                pltpu.make_async_copy(spot, spot, recv.at[number, head, block]).wait()
+            count = (block + 1) * rows
+            o_buf[head, block] = attend(
+                q_buf[head, block],
                 past_k[:, at],
                 past_v[:, at],
-                k_buf[: block + 1, :, at].reshape(count, HEAD),
-                v_buf[: block + 1, :, at].reshape(count, HEAD),
+                k_buf[head, : block + 1].reshape(count, HEAD),
+                v_buf[head, : block + 1].reshape(count, HEAD),
             )
 
-        @pl.when(me != block)
-        def _():
-            pltpu.make_async_remote_copy(
-                src_ref=o_buf.at[block], dst_ref=o_ref.at[:, columns(me)],
-                send_sem=o_send.at[block], recv_sem=o_recv.at[me],
-                device_id={"seq": block}, device_id_type=pl.DeviceIdType.MESH,
-            ).start()
-
-        @pl.when(me == block)
-        def _():
-            pltpu.make_async_copy(o_buf.at[block], o_ref.at[:, columns(me)], o_recv.at[me]).start()
+            @pl.when(me != block)
+            def _():
+                pltpu.make_async_remote_copy(
+                    src_ref=o_buf.at[head, block], dst_ref=o_ref.at[:, lanes(me, head)],
+                    send_sem=o_send.at[head, block], recv_sem=o_recv.at[head, me],
+                    device_id={"seq": block}, device_id_type=pl.DeviceIdType.MESH,
+                ).start()
+
+            @pl.when(me == block)
+            def _():
+                pltpu.make_async_copy(
+                    o_buf.at[head, block], o_ref.at[:, lanes(me, head)], o_recv.at[head, me]
+                ).start()
 
     for copy in sent:
         copy.wait_send()
-    for block in range(seqs):
-        spot = o_ref.at[:, block * width : (block + 1) * width]
-        pltpu.make_async_copy(spot, spot, o_recv.at[block]).wait()
-
-        @pl.when(me != block)
-        def _():
-            pltpu.make_async_copy(o_buf.at[block], o_buf.at[block], o_send.at[block]).wait()
+    for head in range(heads):
+        for block in range(seqs):
+            spot = o_ref.at[:, lanes(block, head)]
+            pltpu.make_async_copy(spot, spot, o_recv.at[head, block]).wait()
+
+            @pl.when(me != block)
+            def _():
+                spot = o_buf.at[head, block]
+                pltpu.make_async_copy(spot, spot, o_send.at[head, block]).wait()
 
 
 def local_kernel(seqs, tps, att_query, att_key, att_value, past_key, past_value):
@@ -290,18 +307,18 @@
             pltpu.VMEM((seqs, tps, 2 * past_rows, width), bf16),
             pltpu.VMEM((depth, width), bf16),
             pltpu.VMEM((depth, width), bf16),
-            pltpu.VMEM((seqs, rows, width), bf16),
-            pltpu.VMEM((seqs, rows, width), bf16),
-            pltpu.VMEM((seqs, rows, width), bf16),
-            pltpu.VMEM((seqs, rows, width), bf16),
+            pltpu.VMEM((width // HEAD, seqs, rows, HEAD), bf16),
+            pltpu.VMEM((width // HEAD, seqs, rows, HEAD), bf16),
+            pltpu.VMEM((width // HEAD, seqs, rows, HEAD), bf16),
+            pltpu.VMEM((width // HEAD, seqs, rows, HEAD), bf16),
             dma((tps,)),
             dma((tps,)),
             dma((seqs,)),
             dma((seqs,)),
-            dma((3, seqs)),
-            dma((3, seqs)),
-            dma((seqs,)),
-            dma((seqs,)),
+            dma((3, width // HEAD, seqs)),
+            dma((3, width // HEAD, seqs)),
+            dma((width // HEAD, seqs)),
+            dma((width // HEAD, seqs)),
         ],
         compiler_params=pltpu.CompilerParams(
             collective_id=0, has_side_effects=True, vmem_limit_bytes=56 * 2**20

time: 64.3 us -> 61.3 us (0.953)
  the two profiles are of different devices: /device:TPU:30 before, /device:TPU:0 now
where the time goes in v8:
time: 61.3 us; the launch traced here: 61.1 us
  Pallas kernels  59.2 us (97%)
  local copies, waits for them, and re-layouts  1.88 us (3%)
    pallas_call x1, Pallas kernels, local_kernel(): pl.pallas_call(functools.partial(exchange_kernel, seqs, tps), out_shape=j...  59.2 us
    unnamed x1, local copies, waits for them, and re-layouts  1.88 us

profile of v8, /device:TPU:0, one launch (start us, length us, event | category | flops | bytes accessed | tf_op | source)
XLA Modules:
  0.0 61.1 jit_solution(15557348177558233797)
XLA Ops:
  0.0 59.2 %shard_map.55 = bf16[128,2048]{1,0:T(8,128)(2,1)} custom-call(bf16[128,2048]{1,0:T(8,128)(2,1)} %q_ref.1, bf16[128,2048]{1,0:T(8,128)(2,1)} %k_ref.1, bf16[128,2048]{1,0:T(8,128)(2,1)} %v_ref.1, bf16[8,8192]{1,0:T(8,128)(2,1)} %pk_ref.1, bf16[8,8192]{1,0:T(8,128)(2,1)} %pv_ref.1), custom_call_target="tpu_custom_call" | custom-call | tf_op jit(solution)/shard_map/pallas_call | solution.py:299
  59.2 1.9 %copy.7 = bf16[128,2048]{1,0:T(8,128)(2,1)} copy(bf16[128,2048]{1,0:T(8,128)(2,1)} %shard_map.55) | data formatting | bytes 1048576
